TPU v7x, 32 devices: a whole 2x2x4 slice. The times are simulated.
32 devices in a mesh: az: 8 (over y, x, core), rad: 4 (over z).
Axes of the slice: x: 2, y: 2, z: 4, core: 2. Of those that a mesh axis runs over, the one named last changes fastest.
Arguments:
- density: float32 [4, 128, 512], P(None, 'az', 'rad'), may hold values from 1 to 2
- momentum: float32 [3, 4, 128, 512], P(None, None, 'az', 'rad'), may hold values from -2.5 to 2.5
- magnetic: float32 [3, 4, 128, 512], P(None, None, 'az', 'rad'), may hold values from -3 to 3
- tracer: float32 [4, 128, 512], P(None, 'az', 'rad'), may hold values from 0 to 1
- shear_offset: int32 [2], replicated, may hold values from 0 to 79, as said below
Outputs:
- new_state: float32 [8, 4, 128, 512], P(None, None, 'az', 'rad')
Inputs may be any that keep to these rules, and one draw needn't show every extreme that they name: shear_offset[0] is below 16; shear_offset[1] is 64 plus a whole number below 16.
All inputs are finite; a program needn't handle non-finite values.
Results may differ from a plain program's by a relative error of at most 0.00002.
Values sent between devices are 32-bit elements; how exact they have to be, the bound alone decides.
No kernel may reach another device: no remote copies, remote signals or barrier semaphores. Data moves between devices by JAX's collectives and lax.ppermute only.
A program may use at most 64 MiB of HBM per device.

v0:
```python
import jax
import jax.numpy as jnp
from jax import lax
from jax.sharding import PartitionSpec as P

time_step = 0.025
viscosity = 0.5
sound_squared = 1.0
shear_speed = 1.0
frac_weight = 0.375


def with_halo(cells, sides, width):
    for axis, dim in sides:
        count = lax.axis_size(axis)
        head = lax.slice_in_dim(cells, 0, width, axis=dim)
        tail = lax.slice_in_dim(cells, cells.shape[dim] - width, cells.shape[dim], axis=dim)
        cells = jnp.concatenate(
            [
                lax.ppermute(tail, axis, [(i, (i + 1) % count) for i in range(count)]),
                cells,
                lax.ppermute(head, axis, [((i + 1) % count, i) for i in range(count)]),
            ],
            axis=dim,
        )
    return cells


def fluxes(padded, direction):
    density_part = padded[0]
    velocity = [padded[1 + component] / density_part for component in range(3)]
    field_part = [padded[4 + component] for component in range(3)]
    pressure = sound_squared * density_part + 0.5 * (
        field_part[0] * field_part[0]
        + field_part[1] * field_part[1]
        + field_part[2] * field_part[2]
    )
    normal_vel = velocity[direction]
    normal_mag = field_part[direction]
    result = [padded[1 + direction]]
    for component in range(3):
        summand = padded[1 + component] * normal_vel - field_part[component] * normal_mag
        if component == direction:
            summand = summand + pressure
        result.append(summand)
    for component in range(3):
        result.append(normal_vel * field_part[component] - normal_mag * velocity[component])
    result.append(padded[7] * normal_vel)
    return jnp.stack(result)


def offset_slice(padded, along, length, shift_by):
    return lax.slice_in_dim(padded, 3 + shift_by, 3 + shift_by + length, axis=along)


def central(padded, along, length):
    return (
        45.0 * (offset_slice(padded, along, length, 1) - offset_slice(padded, along, length, -1))
        - 9.0 * (offset_slice(padded, along, length, 2) - offset_slice(padded, along, length, -2))
        + (offset_slice(padded, along, length, 3) - offset_slice(padded, along, length, -3))
    ) / 60.0


def second(padded, along, length):
    return (
        offset_slice(padded, along, length, 1)
        - 2.0 * offset_slice(padded, along, length, 0)
        + offset_slice(padded, along, length, -1)
    )


def tendency(row_padded, col_padded):
    row_count = row_padded.shape[2] - 6
    col_count = col_padded.shape[3] - 6
    core_rows = row_padded[:, :, 3 : 3 + row_count]
    vertical_pad = jnp.concatenate([core_rows[:, -3:], core_rows, core_rows[:, :3]], axis=1)
    layer_count = core_rows.shape[1]
    summed = -(
        central(fluxes(col_padded, 0), 3, col_count)
        + central(fluxes(row_padded, 1), 2, row_count)
        + central(fluxes(vertical_pad, 2), 1, layer_count)
    )
    summed = summed + viscosity * (
        second(col_padded, 3, col_count)
        + second(row_padded, 2, row_count)
        + second(vertical_pad, 1, layer_count)
    )
    return summed


def blend_rows(window, row_count, lead_weight, trail_weight, jump_sign):
    blended = (
        lead_weight * window[:, :, :row_count] + trail_weight * window[:, :, 1 : row_count + 1]
    )
    return jnp.concatenate(
        [blended[:2], blended[2:3] + jump_sign * shear_speed * blended[0:1], blended[3:]], axis=0
    )


def pack_pair(paired):
    return jnp.moveaxis(paired, 4, 2).reshape(paired.shape[0], paired.shape[1], paired.shape[4], -1)


def sheared(inner_src, outer_src, offset, own_rows):
    layers = inner_src.shape[1]
    src_rows = inner_src.shape[2]
    halo_rows = (src_rows - own_rows) // 2
    window_rows = own_rows + 2 * halo_rows
    total_rows = own_rows * lax.axis_size("az")
    starts = [offset, total_rows - 1 - offset]
    paired = jnp.stack([inner_src, outer_src])
    windows = []
    flat_pair = pack_pair(paired).reshape(1, -1)
    collected = lax.all_gather(flat_pair, "az", axis=0, tiled=True)
    count = collected.shape[0]
    spread = collected.reshape(count, 2, paired.shape[1], 3, layers, own_rows)
    gathered = jnp.transpose(spread, (1, 2, 4, 0, 5, 3)).reshape(
        2, paired.shape[1], layers, count * own_rows, 3
    )
    extended = jnp.concatenate([gathered, gathered[:, :, :, : window_rows + 1]], axis=3)
    first_row = lax.axis_index("az") * own_rows - halo_rows
    for side_index in range(2):
        windows.append(
            lax.dynamic_slice_in_dim(
                extended[side_index],
                (first_row + starts[side_index]) % total_rows,
                window_rows + 1,
                2,
            )
        )
    inner_ghost = blend_rows(windows[0], window_rows, 1.0 - frac_weight, frac_weight, 1.0)
    outer_ghost = blend_rows(windows[1], window_rows, frac_weight, 1.0 - frac_weight, -1.0)
    return (inner_ghost, outer_ghost)


def radial_pad(source, offset, own_rows):
    layers = source.shape[1]
    rows = source.shape[2]
    edges = jnp.concatenate([source[..., :3], source[..., -3:]], axis=3)
    flat_edges = jnp.moveaxis(edges, 3, 1).reshape(source.shape[0], 6, -1)
    arrived = with_halo(flat_edges, (("rad", 1),), 3)
    columns = jnp.moveaxis(arrived.reshape(source.shape[0], 12, layers, rows), 1, 3)
    inner_src = columns[..., :3]
    outer_src = columns[..., -3:]
    inner_ghost, outer_ghost = sheared(inner_src, outer_src, offset, own_rows)
    position = lax.axis_index("rad")
    last_index = lax.axis_size("rad") - 1
    left_cols = jnp.where(position == 0, inner_ghost, inner_src)
    right_cols = jnp.where(position == last_index, outer_ghost, outer_src)
    return jnp.concatenate([left_cols, source, right_cols], axis=3)


def shards(density, momentum, magnetic, tracer, shear_offset):
    conserved = jnp.concatenate([density[None], momentum, magnetic, tracer[None]], axis=0)
    own_rows = conserved.shape[2]
    current = conserved
    for section_index in range(2):
        row_padded = with_halo(current, (("az", 2),), 3)
        current = current + time_step * tendency(
            row_padded, radial_pad(current, shear_offset[section_index], own_rows)
        )
    return 0.5 * conserved + 0.5 * current


def solution(mesh):
    placed = (
        P(None, "az", "rad"),
        P(None, None, "az", "rad"),
        P(None, None, "az", "rad"),
        P(None, "az", "rad"),
        P(),
    )
    return jax.shard_map(
        shards, mesh=mesh, in_specs=placed, out_specs=P(None, None, "az", "rad"), check_vma=False
    )
```

profile of v0, /device:TPU:0, one launch (start us, length us, event | category | flops | bytes accessed | tf_op | source)
XLA Modules:
  0.0 50.9 jit_solution(3777332604085854544)
XLA Ops:
  0.0 1.0 %pad_maximum_fusion.36 = f32[8,4,16,128]{3,2,1,0:T(8,128)S(1)} fusion(f32[1,4,16,128]{3,2,1,0:T(8,128)} %bitcast.62, f32[3,4,16,128]{3,2,1,0:T(8,128)} %param.7, f32[3,4,16,128]{3,2,1,0:T(8,128)} %param.6, f32[1,4,16,128]{3,2,1,0:T(8,128)} %bitcast.68), kind=kLoop, calls=%fused_computation.112 | loop fusion | flops 196608 | bytes 524288 | tf_op jit(solution)/shard_map/concatenate | solution.py:154
  1.0 0.5 collective-permute-start.2
  1.6 3.0 %collective-permute-start.3 = (f32[8,4,3,128]{3,0,2,1:T(8,128)S(1)}, f32[8,4,3,128]{3,0,2,1:T(8,128)S(1)}, u32[]{:S(2)}, u32[]{:S(2)}) collective-permute-start(f32[8,4,3,128]{3,0,2,1:T(8,128)S(1)} %copy.319), channel_id=1, source_target_pairs={{4,0},{8,4},{12,8},{16,12},{20,16},{24,20},{28,24},{0,28},{5,1},{9... | collective-permute-start | bytes 147464 | tf_op jit(solution)/shard_map/ppermute | solution.py:22
  4.7 0.3 copy.284
  4.9 0.3 copy.285
  5.4 2.4 %collective-permute-start = (f32[8,3,64]{2,0,1:T(8,128)S(1)}, f32[8,3,64]{2,0,1:T(8,128)S(1)}, u32[]{:S(2)}, u32[]{:S(2)}) collective-permute-start(f32[8,3,64]{2,0,1:T(8,128)S(1)} %get-tuple-element.39), channel_id=1, source_target_pairs={{0,1},{1,2},{2,3},{3,0},{4,5},{5,6},{6,7},{7,4},{8,9},{9,10},{10,1... | collective-permute-start | bytes 18440 | tf_op jit(solution)/shard_map/ppermute | solution.py:20
  7.8 2.1 %collective-permute-start.1 = (f32[8,3,64]{2,0,1:T(8,128)S(1)}, f32[8,3,64]{2,0,1:T(8,128)S(1)}, u32[]{:S(2)}, u32[]{:S(2)}) collective-permute-start(f32[8,3,64]{2,0,1:T(8,128)S(1)} %get-tuple-element.40), channel_id=1, source_target_pairs={{1,0},{2,1},{3,2},{0,3},{5,4},{6,5},{7,6},{4,7},{9,8},{10,9},{11,1... | collective-permute-start | bytes 18440 | tf_op jit(solution)/shard_map/ppermute | solution.py:22
  10.3 0.6 %copy-done.4 = s32[2]{0:T(128)S(1)} copy-done((s32[2]{0:T(128)S(1)}, s32[2]{0:T(128)}, u32[]{:S(2)}) %copy-start.4) | copy-done | bytes 32
  10.9 0.6 %fusion.76 = (s32[1]{0:T(128)}, s32[1]{0:T(128)}) fusion(s32[2]{0:T(128)S(1)} %copy-done.4), kind=kLoop, calls=%fused_computation.229 | loop fusion | bytes 16 | tf_op jit(solution)/shard_map/slice | solution.py:160
  14.7 9.4 %all-gather = f32[8,1,3072]{2,1,0:T(1,128)S(1)} all-gather(f32[1,1,3072]{2,1,0:T(1,128)S(1)} %reshape.38), channel_id=1, replica_groups=mesh['az'=8,'rad'=4] {'az'}, dimensions={0}, use_global_device_ids=true | all-gather | bytes 110592 | tf_op jit(solution)/shard_map/all_gather | solution.py:114
  24.3 0.6 %reshape.33 = f32[8,2,8,3,4,16]{5,4,3,2,1,0:T(4,128)S(1)} reshape(f32[8,3072]{1,0:T(8,128)S(1)} %reduce) | data formatting | bytes 196608 | tf_op jit(solution)/shard_map/reshape | solution.py:116
  24.9 0.5 copy.290
  25.4 0.2 reshape.34
  26.2 0.3 copy.292
  26.4 0.3 copy.291
  26.7 0.3 pad_maximum_fusion.2
  27.5 0.7 %fusion.34 = f32[8,4,16,128]{3,2,1,0:T(8,128)S(1)} fusion(f32[8,3,16,128]{3,2,1,0:T(8,128)S(1)} %get-tuple-element.28, f32[1,4,16,128]{3,2,1,0:T(8,128)S(1)} %bitcast.66, f32[3,4,16,128]{3,2,1,0:T(8,128)S(1)} %copy-done, f32[3,4,16,128]{3,2,1,0:T(8,128)S(1)} %copy-done.1, f32[1,4,16,128]{3,2,1,0:T(8,128)S(1)} %bitcast.72, ...), kind=kLoop, calls=%fused_computation.57 | loop fusion | flops 4259840 | bytes 5746688 | tf_op jit(solution)/shard_map/add | solution.py:159
  28.5 0.4 collective-permute-start.6
  28.9 2.3 %collective-permute-start.7 = (f32[8,4,3,128]{3,0,2,1:T(8,128)S(1)}, f32[8,4,3,128]{3,0,2,1:T(8,128)S(1)}, u32[]{:S(2)}, u32[]{:S(2)}) collective-permute-start(f32[8,4,3,128]{3,0,2,1:T(8,128)S(1)} %copy.311), channel_id=1, source_target_pairs={{4,0},{8,4},{12,8},{16,12},{20,16},{24,20},{28,24},{0,28},{5,1},{9... | collective-permute-start | bytes 147464 | tf_op jit(solution)/shard_map/ppermute | solution.py:22
  31.2 0.2 copy.301
  31.4 0.3 copy.302
  32.1 3.7 %collective-permute-start.5 = (f32[8,3,64]{2,0,1:T(8,128)S(1)}, f32[8,3,64]{2,0,1:T(8,128)S(1)}, u32[]{:S(2)}, u32[]{:S(2)}) collective-permute-start(f32[8,3,64]{2,0,1:T(8,128)S(1)} %get-tuple-element.38), channel_id=1, source_target_pairs={{1,0},{2,1},{3,2},{0,3},{5,4},{6,5},{7,6},{4,7},{9,8},{10,9},{11,1... | collective-permute-start | bytes 18440 | tf_op jit(solution)/shard_map/ppermute | solution.py:22
  36.1 1.1 %collective-permute-done.5 = f32[8,3,64]{2,0,1:T(8,128)S(1)} collective-permute-done((f32[8,3,64]{2,0,1:T(8,128)S(1)}, f32[8,3,64]{2,0,1:T(8,128)S(1)}, u32[]{:S(2)}, u32[]{:S(2)}) %collective-permute-start.5) | collective-permute-done | bytes 6176 | tf_op jit(solution)/shard_map/ppermute | solution.py:22
  37.8 8.3 %all-gather.1 = f32[8,1,3072]{2,1,0:T(1,128)S(1)} all-gather(f32[1,1,3072]{2,1,0:T(1,128)S(1)} %reshape.40), channel_id=1, replica_groups=mesh['az'=8,'rad'=4] {'az'}, dimensions={0}, use_global_device_ids=true | all-gather | bytes 110592 | tf_op jit(solution)/shard_map/all_gather | solution.py:114
  46.1 0.2 reduce.1
  46.3 0.6 %reshape.36 = f32[8,2,8,3,4,16]{5,4,3,2,1,0:T(4,128)S(1)} reshape(f32[8,3072]{1,0:T(8,128)S(1)} %reduce.1) | data formatting | bytes 196608 | tf_op jit(solution)/shard_map/reshape | solution.py:116
  46.9 0.5 copy.307
  47.4 0.2 reshape.37
  48.2 0.3 copy.309
  48.4 0.3 copy.308
  48.7 0.3 pad_maximum_fusion.3
  49.5 1.4 %fusion.7 = f32[8,4,16,128]{3,2,1,0:T(8,128)} fusion(f32[8,4,16,128]{3,2,1,0:T(8,128)S(1)} %fusion.34, f32[8,3,16,128]{3,2,1,0:T(8,128)S(1)} %get-tuple-element.22, f32[8,3,16,128]{3,2,1,0:T(8,128)S(1)} %get-tuple-element.21, f32[8,4,3,128]{3,2,1,0:T(4,128)S(1)} %copy.312, f32[8,4,3,128]{3,2,1,0:T(4,128)S(1)} %copy.313, f32[8,4,16,3]{3,2,1,0:T(8,128)S(1)} %copy.308, ...), kind=kLoop, calls=%fused_computation.14 | loop fusion | flops 3211264 | bytes 6008832 | tf_op jit(solution)/shard_map/add | solution.py:162
  (135 shorter events, 4.3 us)
Async XLA Ops:
  1.0 26.1 %collective-permute-start.2 = (f32[8,4,3,128]{3,0,2,1:T(8,128)S(1)}, f32[8,4,3,128]{3,0,2,1:T(8,128)S(1)}, u32[]{:S(2)}, u32[]{:S(2)}) collective-permute-start(f32[8,4,3,128]{3,0,2,1:T(8,128)S(1)} %copy.318), channel_id=1, source_target_pairs={{0,4},{4,8},{8,12},{12,16},{16,20},{20,24},{24,28},{28,0},{1,5},{5... | collective-permute-start | bytes 147464 | tf_op jit(solution)/shard_map/ppermute | solution.py:20
  1.6 25.7 %collective-permute-start.3 = (f32[8,4,3,128]{3,0,2,1:T(8,128)S(1)}, f32[8,4,3,128]{3,0,2,1:T(8,128)S(1)}, u32[]{:S(2)}, u32[]{:S(2)}) collective-permute-start(f32[8,4,3,128]{3,0,2,1:T(8,128)S(1)} %copy.319), channel_id=1, source_target_pairs={{4,0},{8,4},{12,8},{16,12},{20,16},{24,20},{28,24},{0,28},{5,1},{9... | collective-permute-start | bytes 147464 | tf_op jit(solution)/shard_map/ppermute | solution.py:22
  5.4 9.0 %collective-permute-start = (f32[8,3,64]{2,0,1:T(8,128)S(1)}, f32[8,3,64]{2,0,1:T(8,128)S(1)}, u32[]{:S(2)}, u32[]{:S(2)}) collective-permute-start(f32[8,3,64]{2,0,1:T(8,128)S(1)} %get-tuple-element.39), channel_id=1, source_target_pairs={{0,1},{1,2},{2,3},{3,0},{4,5},{5,6},{6,7},{7,4},{8,9},{9,10},{10,1... | collective-permute-start | bytes 18440 | tf_op jit(solution)/shard_map/ppermute | solution.py:20
  7.8 2.2 %copy-start = (f32[3,4,16,128]{3,2,1,0:T(8,128)S(1)}, f32[3,4,16,128]{3,2,1,0:T(8,128)}, u32[]{:S(2)}) copy-start(f32[3,4,16,128]{3,2,1,0:T(8,128)} %param.7) | copy-start | bytes 294916
  7.8 2.2 %copy-start.1 = (f32[3,4,16,128]{3,2,1,0:T(8,128)S(1)}, f32[3,4,16,128]{3,2,1,0:T(8,128)}, u32[]{:S(2)}) copy-start(f32[3,4,16,128]{3,2,1,0:T(8,128)} %param.6) | copy-start | bytes 294916
  7.8 2.2 %copy-start.2 = (f32[4,16,128]{2,1,0:T(8,128)S(1)}, f32[4,16,128]{2,1,0:T(8,128)}, u32[]{:S(2)}) copy-start(f32[4,16,128]{2,1,0:T(8,128)} %param.8) | copy-start | bytes 98308
  7.8 2.2 %copy-start.3 = (f32[4,16,128]{2,1,0:T(8,128)S(1)}, f32[4,16,128]{2,1,0:T(8,128)}, u32[]{:S(2)}) copy-start(f32[4,16,128]{2,1,0:T(8,128)} %param.5) | copy-start | bytes 98308
  7.8 6.5 %collective-permute-start.1 = (f32[8,3,64]{2,0,1:T(8,128)S(1)}, f32[8,3,64]{2,0,1:T(8,128)S(1)}, u32[]{:S(2)}, u32[]{:S(2)}) collective-permute-start(f32[8,3,64]{2,0,1:T(8,128)S(1)} %get-tuple-element.40), channel_id=1, source_target_pairs={{1,0},{2,1},{3,2},{0,3},{5,4},{6,5},{7,6},{4,7},{9,8},{10,9},{11,1... | collective-permute-start | bytes 18440 | tf_op jit(solution)/shard_map/ppermute | solution.py:22
  10.3 0.7 %copy-start.4 = (s32[2]{0:T(128)S(1)}, s32[2]{0:T(128)}, u32[]{:S(2)}) copy-start(s32[2]{0:T(128)} %param.9) | copy-start | bytes 28
  28.5 20.7 %collective-permute-start.6 = (f32[8,4,3,128]{3,0,2,1:T(8,128)S(1)}, f32[8,4,3,128]{3,0,2,1:T(8,128)S(1)}, u32[]{:S(2)}, u32[]{:S(2)}) collective-permute-start(f32[8,4,3,128]{3,0,2,1:T(8,128)S(1)} %copy.310), channel_id=1, source_target_pairs={{0,4},{4,8},{8,12},{12,16},{16,20},{20,24},{24,28},{28,0},{1,5},{5... | collective-permute-start | bytes 147464 | tf_op jit(solution)/shard_map/ppermute | solution.py:20
  28.9 20.4 %collective-permute-start.7 = (f32[8,4,3,128]{3,0,2,1:T(8,128)S(1)}, f32[8,4,3,128]{3,0,2,1:T(8,128)S(1)}, u32[]{:S(2)}, u32[]{:S(2)}) collective-permute-start(f32[8,4,3,128]{3,0,2,1:T(8,128)S(1)} %copy.311), channel_id=1, source_target_pairs={{4,0},{8,4},{12,8},{16,12},{20,16},{24,20},{28,24},{0,28},{5,1},{9... | collective-permute-start | bytes 147464 | tf_op jit(solution)/shard_map/ppermute | solution.py:22
  31.9 5.5 %collective-permute-start.4 = (f32[8,3,64]{2,0,1:T(8,128)S(1)}, f32[8,3,64]{2,0,1:T(8,128)S(1)}, u32[]{:S(2)}, u32[]{:S(2)}) collective-permute-start(f32[8,3,64]{2,0,1:T(8,128)S(1)} %get-tuple-element.37), channel_id=1, source_target_pairs={{0,1},{1,2},{2,3},{3,0},{4,5},{5,6},{6,7},{7,4},{8,9},{9,10},{10,1... | collective-permute-start | bytes 18440 | tf_op jit(solution)/shard_map/ppermute | solution.py:20
  32.1 5.1 %collective-permute-start.5 = (f32[8,3,64]{2,0,1:T(8,128)S(1)}, f32[8,3,64]{2,0,1:T(8,128)S(1)}, u32[]{:S(2)}, u32[]{:S(2)}) collective-permute-start(f32[8,3,64]{2,0,1:T(8,128)S(1)} %get-tuple-element.38), channel_id=1, source_target_pairs={{1,0},{2,1},{3,2},{0,3},{5,4},{6,5},{7,6},{4,7},{9,8},{10,9},{11,1... | collective-permute-start | bytes 18440 | tf_op jit(solution)/shard_map/ppermute | solution.py:22
where the time goes:
time: 51.2 us; the launch traced here: 50.9 us
  blocking collectives  17.7 us (35%)
  starting transfers between devices  14.5 us (28%)
  local copies, waits for them, and re-layouts  7.47 us (15%)
  other arithmetic  6.18 us (12%)
  between operations  3.75 us (7%)
  waiting for transfers between devices  1.28 us (2%)
    all_gather x2, blocking collectives, sheared(): collected = lax.all_gather(flat_pair, 'az', axis=0, tiled=True)  17.7 us
    ppermute x4, starting transfers between devices, with_halo(): lax.ppermute(head, axis, [((i + 1) % count, i) for i in range(count)])  11.1 us
    ppermute x4, starting transfers between devices, with_halo(): lax.ppermute(tail, axis, [(i, (i + 1) % count) for i in range(count)])  3.46 us
    add x1, other arithmetic, shards(): return 0.5 * conserved + 0.5 * current  1.42 us
    slice x6, local copies, waits for them, and re-layouts, radial_pad(): edges = jnp.concatenate([source[..., :3], source[..., -3:]], axis=3)  1.3 us
    reshape x2, local copies, waits for them, and re-layouts, sheared(): spread = collected.reshape(count, 2, paired.shape[1], 3, layers, own_rows)  1.13 us
    ppermute x4, waiting for transfers between devices, with_halo(): lax.ppermute(head, axis, [((i + 1) % count, i) for i in range(count)])  1.11 us
  transfers between devices with their start and end apart: 8, of which 2 were waited for; matrix products, arithmetic and copies ran while one was open for 18% of the time, Pallas kernels for 0%

commit v1 on v0

v1 whole, which is shorter than its diff:
```python
import functools

import jax
import jax.numpy as jnp
from jax import lax
from jax.experimental import pallas as pl
from jax.experimental.pallas import tpu as pltpu
from jax.sharding import PartitionSpec as P

time_step = 0.025
viscosity = 0.5
sound_squared = 1.0
shear_speed = 1.0
frac_weight = 0.375
stencil = ((1, 45.0 / 60.0), (2, -9.0 / 60.0), (3, 1.0 / 60.0))
REACH = 3
FIELDS = 8
SUB = 8
RIGHT = 16
PACK = 8


def struct(*shape):
    return jax.ShapeDtypeStruct(shape, jnp.float32)


def lanes_of(shape):
    return lax.broadcasted_iota(jnp.int32, shape, len(shape) - 1)


def move(values, by):
    count = values.shape[-1]
    if isinstance(by, int):
        by = by % count
        return values if by == 0 else pltpu.roll(values, by, values.ndim - 1)
    return pltpu.roll(values, lax.rem(by + count, count), values.ndim - 1)


def primitives(cells):
    inverse = 1.0 / cells[0]
    velocity = [cells[1 + i] * inverse for i in range(3)]
    squares = cells[4] * cells[4] + cells[5] * cells[5] + cells[6] * cells[6]
    return velocity, sound_squared * cells[0] + 0.5 * squares


def flux(cells, velocity, pressure, direction):
    speed, normal = velocity[direction], cells[4 + direction]
    result = [cells[1 + direction]]
    for i in range(3):
        term = cells[1 + i] * speed - cells[4 + i] * normal
        result.append(term + pressure if i == direction else term)
    for i in range(3):
        result.append(None if i == direction else speed * cells[4 + i] - normal * velocity[i])
    result.append(cells[7] * speed)
    return result


def along_lanes(values, flows, lane, halo_values=None, halo_flows=None):
    count = values.shape[-1]

    def ends(array, halo, width):
        if halo is None:
            return array, array
        return jnp.where(lane < width, halo, array), jnp.where(lane >= count - width, halo, array)

    above, below = ends(values, halo_values, 1)
    up, down = viscosity * above, viscosity * below
    if flows is None:
        return move(up, -1) + move(down, 1)
    total = None
    for distance, weight in stencil:
        above, below = ends(flows, halo_flows, distance)
        plus, minus = -weight * above, weight * below
        if distance == 1:
            plus, minus = plus + up, minus + down
        pair = move(plus, -distance) + move(minus, distance)
        total = pair if total is None else total + pair
    return total


def layer_weights(layers):
    folded = {}
    for distance, weight in stencil:
        for signed, share in ((distance, weight), (-distance, -weight)):
            folded[signed % layers] = folded.get(signed % layers, 0.0) + share
    return {distance: weight for distance, weight in folded.items() if weight != 0.0 and distance != 0}


def strip_section(cells, flows_ref, cells_ref, layers):
    rows, count = cells[0].shape
    slot = count // layers
    velocity, pressure = primitives(cells)
    flow_x, flow_y, flow_z = (flux(cells, velocity, pressure, d) for d in range(3))
    weights = layer_weights(layers)
    result = []
    for f in range(FIELDS):
        total = along_lanes(cells[f], flow_x[f], None)
        total = total + viscosity * (move(cells[f], slot) + move(cells[f], -slot))
        if flow_z[f] is not None:
            for distance, weight in weights.items():
                total = total - weight * move(flow_z[f], -distance * slot)
        cells_ref[SUB : SUB + rows] = cells[f]
        total = total + viscosity * (cells_ref[SUB - 1 : SUB - 1 + rows] + cells_ref[SUB + 1 : SUB + 1 + rows])
        if flow_y[f] is not None:
            flows_ref[SUB : SUB + rows] = flow_y[f]
            for distance, weight in stencil:
                total = total - weight * (
                    flows_ref[SUB + distance : SUB + distance + rows]
                    - flows_ref[SUB - distance : SUB - distance + rows]
                )
        total = total - 6.0 * viscosity * cells[f]
        result.append(cells[f] + time_step * total)
    return result


def sheared(lead, trail, inner):
    first = jnp.where(inner, 1.0 - frac_weight, frac_weight)
    jump = jnp.where(inner, shear_speed, -shear_speed)
    ghosts = [first * a + (1.0 - first) * b for a, b in zip(lead, trail)]
    ghosts[2] = ghosts[2] + jump * ghosts[0]
    return ghosts


def split_pairs(pairs):
    return [pairs[f // 2] if f % 2 == 0 else move(pairs[f // 2], -RIGHT) for f in range(FIELDS)]


def fill_window(window_ref, before_ref, own_ref, after_ref):
    rows = own_ref.shape[1]
    for part, ref in enumerate((before_ref, own_ref, after_ref)):
        window_ref[:, SUB + part * rows : SUB + (part + 1) * rows] = ref[...]


def neighbours(first_ref, second_ref, even):
    return jnp.where(even, second_ref[...], first_ref[...]), jnp.where(even, first_ref[...], second_ref[...])


def axis_place(axis):
    place = lax.axis_index(axis)
    return lax.rem(place, 2), place == 0, place == lax.axis_size(axis) - 1


def edges_kernel(density, momentum, magnetic, tracer, state, near, far, pairs):
    layers, rows, cols = density.shape
    slot = cols // layers
    odd, _, last = axis_place("rad")
    lane = lanes_of((rows, cols))
    width = 2 * REACH
    near_parts, far_parts = [jnp.zeros((rows, cols), jnp.float32)] * 2, [jnp.zeros((rows, cols), jnp.float32)] * 2
    pair_parts = [jnp.zeros((rows, cols), jnp.float32)] * 4
    shift_pair = jnp.where(last, REACH, width)
    for f in range(FIELDS):
        for z in range(layers):
            plane = density[z] if f == 0 else tracer[z] if f == 7 else momentum[f - 1, z] if f < 4 else magnetic[f - 4, z]
            state[f, z] = plane
            start = z * slot + (f % 4) * PACK
            inside = (lane >= start) & (lane < start + PACK)
            left, right = move(plane, start), move(plane, start + width)
            near_parts[f // 4] = jnp.where(inside, jnp.where(odd == 1, right, left), near_parts[f // 4])
            far_parts[f // 4] = jnp.where(inside, jnp.where(odd == 1, left, right), far_parts[f // 4])
            start = z * slot + (f % 2) * RIGHT
            begin = start + jnp.where(last, 0, width)
            inside = (lane >= begin) & (lane < begin + REACH)
            pair_parts[f // 2] = jnp.where(inside, move(plane, start + shift_pair), pair_parts[f // 2])
    for part in range(2):
        near[part], far[part] = near_parts[part], far_parts[part]
    for part in range(4):
        pairs[part] = pair_parts[part]


def join_kernel(pairs, received, joined):
    _, _, last = axis_place("rad")
    slot = 2 * RIGHT
    lane = lax.rem(lanes_of(pairs.shape[1:]), slot)
    offset = jnp.where(last, REACH, 0)
    for part in range(4):
        total = pairs[part]
        for f in (2 * part, 2 * part + 1):
            begin = (f % 2) * RIGHT + offset
            inside = (lane >= begin) & (lane < begin + 2 * REACH)
            total = jnp.where(inside, move(received[f // 4], begin - (f % 4) * PACK), total)
        joined[part] = total


def bulk_kernel(state, near, far, halo, first, second):
    odd, _, _ = axis_place("rad")
    odd_az, _, _ = axis_place("az")
    _, layers, rows, cols = state.shape
    slot = cols // layers
    lane = lax.rem(lanes_of((rows, cols)), slot)
    for f in range(FIELDS):
        a, b = far[f // 4], near[f // 4]
        left, right = jnp.where(odd == 1, a, b), jnp.where(odd == 1, b, a)
        left, right = move(left, -(f % 4) * PACK), move(right, RIGHT + REACH - (f % 4) * PACK)
        halo[f] = jnp.where(
            lane < 2 * REACH,
            left,
            jnp.where((lane >= RIGHT + REACH) & (lane < RIGHT + 3 * REACH), right, 0.0),
        )
    tail = pl.multiple_of((1 - odd_az) * (rows - SUB), SUB)
    head = pl.multiple_of(odd_az * (rows - SUB), SUB)
    planes = FIELDS * layers
    for out, start in ((first, tail), (second, head)):
        for f in range(FIELDS):
            for z in range(layers):
                out[f * layers + z] = state[f, z, pl.ds(start, SUB), :]
            out[planes + f] = halo[f, pl.ds(start, SUB), :]


def far_kernel(offsets, own, first, second, packed, window, flows_ref, cells_ref, *, turn, wrap):
    odd_az, _, _ = axis_place("az")
    _, _, last = axis_place("rad")
    tiles, rows, cols = own.shape
    layers = cols // (2 * RIGHT)
    total_rows = rows * lax.axis_size("az")
    before, after = neighbours(first, second, odd_az == 0)
    fill_window(window, before, own, after)
    shift, turned = offsets[0], offsets[1] - total_rows // 2
    height = rows + SUB
    base = SUB + rows
    begin = jnp.where(last, base - REACH - 1 - turned + wrap * rows, base - REACH + turned - wrap * rows)
    edge = jnp.where(
        last, base - REACH - 1 - turned + turn * rows + shift, base - REACH + turned - turn * rows - shift - 1
    )
    cells = split_pairs([window[t, pl.ds(begin, height), :] for t in range(tiles)])
    lead = split_pairs([window[t, pl.ds(edge, height), :] for t in range(tiles)])
    trail = split_pairs([window[t, pl.ds(edge + 1, height), :] for t in range(tiles)])
    lane = lax.rem(lanes_of((height, cols)), 2 * RIGHT)
    ghost_start = jnp.where(last, 0, 2 * REACH)
    ghost_lane = (lane >= ghost_start) & (lane < ghost_start + REACH)
    ghosts = sheared(lead, trail, last)
    cells = [jnp.where(ghost_lane, g, c) for g, c in zip(ghosts, cells)]
    section = strip_section(cells, flows_ref, cells_ref, layers)
    lead, trail = [], []
    for f in range(FIELDS):
        cells_ref[SUB : SUB + height] = section[f]
        lead.append(cells_ref[SUB + REACH : SUB + REACH + rows])
        trail.append(cells_ref[SUB + REACH + 1 : SUB + REACH + 1 + rows])
    ghosts = sheared(lead, trail, jnp.logical_not(last))
    lane = lax.rem(lanes_of((rows, cols)), 2 * RIGHT)
    for part in range(2):
        total = jnp.zeros((rows, cols), jnp.float32)
        for i in range(4):
            inside = (lane >= i * PACK) & (lane < (i + 1) * PACK)
            total = jnp.where(inside, move(ghosts[4 * part + i], i * PACK - REACH), total)
        packed[part] = total


def ends_to_plane(strip, z, layers):
    return move(strip, -(z * (strip.shape[-1] // layers) + 2 * REACH))


def ends_strip(left, right, lane):
    return jnp.where(lane < 2 * REACH, left, right)


def section_tiles(cells_ref, halo_ref, flow_y, flow_z, partial, layers, tiles, first_row, emit):
    cols = cells_ref.shape[-1]
    lane = lanes_of((SUB, cols))
    weights = layer_weights(layers)
    all_tiles = cells_ref.shape[2] // SUB
    for z in range(layers):
        for t in range(all_tiles):
            span = pl.ds(t * SUB, SUB)
            cells = [cells_ref[f, z, span, :] for f in range(FIELDS)]
            velocity, pressure = primitives(cells)
            flows = flux(cells, velocity, pressure, 1)
            for f in range(FIELDS):
                if flows[f] is not None:
                    flow_y[f, z, span, :] = flows[f]
            if t not in tiles:
                continue
            flows = flux(cells, velocity, pressure, 2)
            for f in range(FIELDS):
                if flows[f] is not None:
                    flow_z[f, z, span, :] = flows[f]
            flows = flux(cells, velocity, pressure, 0)
            halo = [ends_to_plane(halo_ref[f, span, :], z, layers) for f in range(FIELDS)]
            velocity, pressure = primitives(halo)
            halo_flows = flux(halo, velocity, pressure, 0)
            for f in range(FIELDS):
                partial[f, z, span, :] = along_lanes(cells[f], flows[f], lane, halo[f], halo_flows[f])
    for z in range(layers):
        for t in tiles:
            start = t * SUB
            for f in range(FIELDS):
                def near(ref, layer, shift, f=f, start=start):
                    return ref[f, layer, pl.ds(start + shift, SUB), :]

                cells = near(cells_ref, z, 0)
                total = partial[f, z, pl.ds(start, SUB), :]
                around = near(cells_ref, z, 1) + near(cells_ref, z, -1)
                around = around + near(cells_ref, (z + 1) % layers, 0) + near(cells_ref, (z - 1) % layers, 0)
                total = total + viscosity * (around - 6.0 * cells)
                if f != 5:
                    for distance, weight in stencil:
                        total = total - weight * (near(flow_y, z, distance) - near(flow_y, z, -distance))
                if f != 6:
                    for distance, weight in weights.items():
                        total = total - weight * near(flow_z, (z + distance) % layers, 0)
                emit(f, z, t, cells, cells + time_step * total)


def first_kernel(
    offsets, state, own, first, second, halo, first_bulk, second_bulk, section, strips,
    cells_ref, window, halo_ref, flow_y, flow_z, partial, flows_ref, strip_ref, *, wrap,
):
    odd_az, _, _ = axis_place("az")
    _, begins, last = axis_place("rad")
    _, layers, rows, cols = state.shape
    slot = cols // layers
    planes = FIELDS * layers
    height = rows + 2 * SUB
    even = odd_az == 0
    for f in range(FIELDS):
        for z in range(layers):
            a, b = first_bulk[f * layers + z], second_bulk[f * layers + z]
            cells_ref[f, z, SUB : 2 * SUB, :] = jnp.where(even, b, a)
            cells_ref[f, z, 2 * SUB : 2 * SUB + rows, :] = state[f, z]
            cells_ref[f, z, 2 * SUB + rows : 3 * SUB + rows, :] = jnp.where(even, a, b)
    before, after = neighbours(first, second, even)
    fill_window(window, before, own, after)
    begin = jnp.where(last, rows - 1 - offsets[0] + wrap * rows, rows + offsets[0] - wrap * rows)
    lead = split_pairs([window[t, pl.ds(begin, height), :] for t in range(own.shape[0])])
    trail = split_pairs([window[t, pl.ds(begin + 1, height), :] for t in range(own.shape[0])])
    ghosts = sheared(lead, trail, begins)
    lane = lax.rem(lanes_of((height, cols)), slot)
    whole = lanes_of((rows, cols))
    strip_cells = []
    for f in range(FIELDS):
        a, b = first_bulk[planes + f], second_bulk[planes + f]
        strip = jnp.concatenate([jnp.where(even, b, a), halo[f], jnp.where(even, a, b)], axis=0)
        own_part = jnp.zeros((rows, cols), jnp.float32)
        for z in range(layers):
            low = z * slot + 2 * REACH
            own_part = jnp.where((whole >= low) & (whole < low + REACH), move(state[f, z], low), own_part)
            low = z * slot + RIGHT
            own_part = jnp.where((whole >= low) & (whole < low + REACH), move(state[f, z], low + REACH), own_part)
        own_part = jnp.concatenate([jnp.zeros((SUB, cols), jnp.float32), own_part, jnp.zeros((SUB, cols), jnp.float32)], axis=0)
        own_lane = ((lane >= 2 * REACH) & (lane < 3 * REACH)) | ((lane >= RIGHT) & (lane < RIGHT + REACH))
        strip_cells.append(jnp.where(own_lane, own_part, strip))
        right = move(strip, 2 * REACH - RIGHT - REACH)
        left = jnp.where(begins, ghosts[f], strip)
        right = jnp.where(last, move(ghosts[f], REACH), right)
        halo_ref[f, SUB : SUB + height, :] = ends_strip(left, right, lane)
    done = strip_section(strip_cells, flows_ref, strip_ref, layers)
    for f in range(FIELDS):
        right = move(done[f], 2 * REACH - RIGHT - REACH)
        strips[f] = ends_strip(done[f], right, lane)[SUB : SUB + rows]

    def emit(f, z, t, cells, value):
        section[f, z, (t - 1) * SUB : t * SUB, :] = value

    tiles = range(1, 1 + height // SUB)
    section_tiles(cells_ref, halo_ref, flow_y, flow_z, partial, layers, tiles, 0, emit)


def second_kernel(state, section, strips, packed, result, halo_ref, flow_y, flow_z, partial):
    _, begins, last = axis_place("rad")
    _, layers, rows, cols = state.shape
    lane = lax.rem(lanes_of((rows, cols)), cols // layers)
    for f in range(FIELDS):
        ghosts = packed[f // 4]
        left = move(ghosts, REACH - (f % 4) * PACK)
        right = move(ghosts, 2 * REACH - (f % 4) * PACK)
        strip = strips[f]
        halo_ref[f, SUB : SUB + rows, :] = ends_strip(
            jnp.where(begins, left, strip), jnp.where(last, right, strip), lane
        )

    def emit(f, z, t, cells, value):
        rows_of = slice((t - 1) * SUB, t * SUB)
        result[f, z, rows_of, :] = 0.5 * state[f, z, rows_of, :] + 0.5 * value

    tiles = range(1, 1 + rows // SUB)
    section_tiles(section, halo_ref, flow_y, flow_z, partial, layers, tiles, 0, emit)


VMEM = pl.BlockSpec(memory_space=pltpu.VMEM)
SMEM = pl.BlockSpec(memory_space=pltpu.SMEM)


def call(kernel, name, outs, *args, scratch=(), flops=0, smem=0):
    many = isinstance(outs, list)
    return pl.pallas_call(
        kernel,
        name=name,
        out_shape=outs,
        in_specs=[SMEM] * smem + [VMEM] * (len(args) - smem),
        out_specs=[VMEM] * len(outs) if many else VMEM,
        scratch_shapes=[pltpu.VMEM(shape, jnp.float32) for shape in scratch],
        compiler_params=pltpu.CompilerParams(vmem_limit_bytes=24 * 2**20),
        cost_estimate=pl.CostEstimate(flops=flops, bytes_accessed=2**18, transcendentals=0),
    )(*args)


def routes(az_count, rad_count, wrap, turn):
    def listed(target):
        pairs = []
        for a in range(az_count):
            for r in range(rad_count):
                to_a, to_r = target(a, r)
                pairs.append((a * rad_count + r, (to_a % az_count) * rad_count + to_r))
        return pairs

    end = rad_count - 1

    def near(a, r):
        if r == 0:
            return a + wrap, end
        if r == end:
            return a - wrap, 0
        return a, r + 1 if r % 2 else r - 1

    def half_turn(a, r):
        extra = -turn if r == 0 else turn if r == end else 0
        return a + az_count // 2 + extra, r

    return (
        listed(near),
        listed(lambda a, r: (a, r ^ 1)),
        listed(lambda a, r: (a ^ 1, r)),
        listed(lambda a, r: (((a + 1) ^ 1) - 1, r)),
        listed(half_turn),
    )


def exchange_and_step(wrap, turned_wrap, offsets, state, near, far, pairs):
    _, layers, rows, cols = state.shape
    turn = turned_wrap - wrap
    near_route, far_route, first_route, second_route, turn_route = routes(
        lax.axis_size("az"), lax.axis_size("rad"), wrap, turn
    )
    axes = ("az", "rad")
    planes = FIELDS * layers
    near_in = lax.ppermute(near, axes, near_route)
    far_in = lax.ppermute(far, axes, far_route)
    own = call(join_kernel, "join", struct(4, rows, cols), pairs, near_in)
    first = lax.ppermute(own, axes, first_route)
    second = lax.ppermute(own, axes, second_route)
    bulk = struct(planes + FIELDS, SUB, cols)
    halo, to_first, to_second = call(
        bulk_kernel, "bulk", [struct(FIELDS, rows, cols), bulk, bulk], state, near_in, far_in
    )
    first_bulk = lax.ppermute(to_first, axes, first_route)
    second_bulk = lax.ppermute(to_second, axes, second_route)
    window = (4, 3 * rows + 2 * SUB, cols)
    packed = call(
        functools.partial(far_kernel, turn=turn, wrap=turned_wrap),
        "far",
        struct(2, rows, cols),
        offsets,
        own,
        first,
        second,
        scratch=[window] + [(rows + 3 * SUB, cols)] * 2,
        smem=1,
    )
    packed = lax.ppermute(packed, axes, turn_route)
    height = rows + 2 * SUB
    padded = (FIELDS, layers, height + 2 * SUB, cols)
    section, strips = call(
        functools.partial(first_kernel, wrap=wrap),
        "first_section",
        [struct(FIELDS, layers, height, cols), struct(FIELDS, rows, cols)],
        offsets,
        state,
        own,
        first,
        second,
        halo,
        first_bulk,
        second_bulk,
        scratch=[padded, window, (FIELDS, height + 2 * SUB, cols), padded, padded, padded]
        + [(height + 2 * SUB, cols)] * 2,
        smem=1,
        flops=2**23,
    )
    return call(
        second_kernel,
        "second_section",
        struct(FIELDS, layers, rows, cols),
        state,
        section,
        strips,
        packed,
        scratch=[(FIELDS, height, cols)] + [(FIELDS, layers, height, cols)] * 3,
        flops=2**22,
    )


def shards(density, momentum, magnetic, tracer, offsets):
    layers, rows, cols = density.shape
    total_rows = rows * lax.axis_size("az")
    state, near, far, pairs = call(
        edges_kernel,
        "edges",
        [struct(FIELDS, layers, rows, cols), struct(2, rows, cols), struct(2, rows, cols), struct(4, rows, cols)],
        density,
        momentum,
        magnetic,
        tracer,
    )
    crosses = (offsets > jnp.array([rows - 4, rows - 4 + total_rows // 2])).astype(jnp.int32)
    branches = [
        functools.partial(exchange_and_step, wrap, turned_wrap) for wrap in range(2) for turned_wrap in range(2)
    ]
    return lax.switch(2 * crosses[0] + crosses[1], branches, offsets, state, near, far, pairs)


def solution(mesh):
    placed = (
        P(None, "az", "rad"),
        P(None, None, "az", "rad"),
        P(None, None, "az", "rad"),
        P(None, "az", "rad"),
        P(),
    )
    return jax.shard_map(
        shards, mesh=mesh, in_specs=placed, out_specs=P(None, None, "az", "rad"), check_vma=False
    )
```

time: 51.2 us -> 30.5 us (0.60)
  blocking collectives: 17.7 us -> 0 us
  waiting for transfers between devices: 1.28 us -> 8.5 us
  other arithmetic: 6.18 us -> 0.01 us
  Pallas kernels: 0 us -> 5.57 us
  starting transfers between devices: 14.5 us -> 9.18 us
  between operations: 3.75 us -> 1.34 us
  local copies, waits for them, and re-layouts: 7.47 us -> 5.24 us
  loops' own time: 0 us -> 0.52 us
    all_gather x2 -> x0, blocking collectives: 17.7 us -> none  [sheared(): collected = lax.all_gather(flat_pair, 'az', axis=0, tiled=True)]
    ppermute x8 -> x7, waiting for transfers between devices: 1.28 us -> 8.5 us  [the longest x1 4.32 us: exchange_and_step(): second = lax.ppermute(own, axes, second_route)]
    pallas_call x0 -> x6, Pallas kernels: none -> 5.57 us  [call(): pl.pallas_call(kernel, name=name, out_shape=outs, in_specs=[SMEM] * smem...]
    ppermute x8 -> x7, starting transfers between devices: 14.5 us -> 9.18 us  [the longest x1 4.55 us: exchange_and_step(): near_in = lax.ppermute(near, axes, near_route)]
    unnamed x20 -> x14, local copies, waits for them, and re-layouts: 0.97 us -> 4.65 us
    add x10 -> x0, other arithmetic: 2.48 us -> none  [the longest x1 1.42 us: shards(): return 0.5 * conserved + 0.5 * current]
    reshape x6 -> x0, local copies, waits for them, and re-layouts: 1.83 us -> none  [the longest x2 1.13 us: sheared(): spread = collected.reshape(count, 2, paired.shape[1], 3, layers, own_rows)]
    concatenate x7 -> x0, other arithmetic: 1.75 us -> none  [the longest x1 0.98 us: shards(): jnp.concatenate([density[None], momentum, magnetic, tracer[None]], axis=0)]
  transfers between devices with their start and end apart: 8 -> 7, of which waited for: 2 -> 4; matrix products, arithmetic and copies ran while one was open for 18% -> 0% of each run, Pallas kernels for 0% -> 14%
where the time goes in v1:
time: 30.5 us; the launch traced here: 30.4 us
  starting transfers between devices  9.18 us (30%)
  waiting for transfers between devices  8.5 us (28%)
  Pallas kernels  5.57 us (18%)
  local copies, waits for them, and re-layouts  5.24 us (17%)
  between operations  1.34 us (4%)
  loops' own time  0.52 us (2%)
    pallas_call x6, Pallas kernels, call(): pl.pallas_call(kernel, name=name, out_shape=outs, in_specs=[SMEM] * smem...  5.57 us
    unnamed x14, local copies, waits for them, and re-layouts  4.65 us
    ppermute x1, starting transfers between devices, exchange_and_step(): near_in = lax.ppermute(near, axes, near_route)  4.55 us
    ppermute x1, waiting for transfers between devices, exchange_and_step(): second = lax.ppermute(own, axes, second_route)  4.32 us
    ppermute x1, waiting for transfers between devices, exchange_and_step(): far_in = lax.ppermute(far, axes, far_route)  2.31 us
    ppermute x1, starting transfers between devices, exchange_and_step(): second_bulk = lax.ppermute(to_second, axes, second_route)  2.11 us
    ppermute x1, waiting for transfers between devices, exchange_and_step(): near_in = lax.ppermute(near, axes, near_route)  1.33 us
    ppermute x1, starting transfers between devices, exchange_and_step(): packed = lax.ppermute(packed, axes, turn_route)  1.17 us
  transfers between devices with their start and end apart: 7, of which 4 were waited for; matrix products, arithmetic and copies ran while one was open for 0% of the time, Pallas kernels for 14%

profile of v1, /device:TPU:0, one launch (start us, length us, event | category | flops | bytes accessed | tf_op | source)
XLA Modules:
  0.0 30.4 jit_solution(13718504054956589798)
XLA Ops:
  0.0 0.9 %copy-done = f32[3,4,16,128]{3,2,1,0:T(8,128)S(1)} copy-done((f32[3,4,16,128]{3,2,1,0:T(8,128)S(1)}, f32[3,4,16,128]{3,2,1,0:T(8,128)}, u32[]{:S(2)}) %copy-start) | copy-done | bytes 98328
  0.9 0.9 %copy-done.1 = f32[3,4,16,128]{3,2,1,0:T(8,128)S(1)} copy-done((f32[3,4,16,128]{3,2,1,0:T(8,128)S(1)}, f32[3,4,16,128]{3,2,1,0:T(8,128)}, u32[]{:S(2)}) %copy-start.1) | copy-done | bytes 98328
  1.8 0.8 %copy-done.2 = f32[4,16,128]{2,1,0:T(8,128)S(1)} copy-done((f32[4,16,128]{2,1,0:T(8,128)S(1)}, f32[4,16,128]{2,1,0:T(8,128)}, u32[]{:S(2)}) %copy-start.2) | copy-done | bytes 32792
  2.5 0.8 %copy-done.3 = f32[4,16,128]{2,1,0:T(8,128)S(1)} copy-done((f32[4,16,128]{2,1,0:T(8,128)S(1)}, f32[4,16,128]{2,1,0:T(8,128)}, u32[]{:S(2)}) %copy-start.3) | copy-done | bytes 32792
  3.3 0.3 edges.1
  3.6 0.0 copy-start.5
  3.6 0.0 copy-start.6
  3.6 0.6 %copy-done.5 = s32[2]{0:T(128)S(1)} copy-done((s32[2]{0:T(128)S(1)}, s32[2]{0:T(128)}, u32[]{:S(2)}) %copy-start.5) | copy-done | bytes 32
  4.2 0.0 copy-done.6
  4.3 0.6 %fusion = (s32[1]{0:T(128)}, s32[1]{0:T(128)}) fusion(s32[2]{0:T(128)S(1)} %compare_convert_fusion), kind=kLoop, calls=%fused_computation.1 | loop fusion | bytes 16 | tf_op jit(solution)/shard_map/slice | solution.py:508
  6.1 23.5 %conditional.1 = (f32[8,4,16,128]{3,2,1,0:T(8,128)S(1)}) conditional(s32[]{:T(128)} %bitcast, (f32[2,16,128]{2,1,0:T(8,128)S(1)}, f32[4,16,128]{2,1,0:T(8,128)S(1)}, f32[2,16,128]{2,1,0:T(8,128)S(1)}, f32[8,4,16,128]{3,2,1,0:T(8,128)S(1)}, s32[2]{0:T(128)S(1)}) %tuple.28, (f32[2,16,128]{2,1,0:T(8,128)S(1)}, ...), branch_computations={%region_0.0_spmd, %region_1.0_spmd, %region_2.0_spmd, %region_3.0_... | conditional | flops 12582912 | bytes 3080480 | solution.py:508
  6.4 4.6 %collective-permute-start.21 = (f32[2,16,128]{2,1,0:T(8,128)S(1)}, f32[2,16,128]{2,1,0:T(8,128)S(1)}, u32[]{:S(2)}, u32[]{:S(2)}) collective-permute-start(f32[2,16,128]{2,1,0:T(8,128)S(1)} %get-tuple-element.83), channel_id=1, source_target_pairs={{0,7},{1,2},{2,1},{3,28},{4,11},{5,6},{6,5},{7,0},{8,15},{9,10},{1... | collective-permute-start | bytes 49160 | tf_op jit(solution)/shard_map/cond/branch_3_fun/ppermute | solution.py:436
  11.0 0.1 collective-permute-start.24
  11.1 1.3 %collective-permute-done.21.received.near = f32[2,16,128]{2,1,0:T(8,128)S(1)} collective-permute-done((f32[2,16,128]{2,1,0:T(8,128)S(1)}, f32[2,16,128]{2,1,0:T(8,128)S(1)}, u32[]{:S(2)}, u32[]{:S(2)}) %collective-permute-start.21) | collective-permute-done | bytes 16416 | tf_op jit(solution)/shard_map/cond/branch_3_fun/ppermute | solution.py:436
  12.4 2.3 %collective-permute-done.24.far = f32[2,16,128]{2,1,0:T(8,128)S(1)} collective-permute-done((f32[2,16,128]{2,1,0:T(8,128)S(1)}, f32[2,16,128]{2,1,0:T(8,128)S(1)}, u32[]{:S(2)}, u32[]{:S(2)}) %collective-permute-start.24) | collective-permute-done | bytes 16416 | tf_op jit(solution)/shard_map/cond/branch_3_fun/ppermute | solution.py:437
  14.7 0.1 bulk.7
  14.8 0.5 %collective-permute-start.25 = (f32[40,8,128]{2,1,0:T(8,128)S(1)}, f32[40,8,128]{2,1,0:T(8,128)S(1)}, u32[]{:S(2)}, u32[]{:S(2)}) collective-permute-start(f32[40,8,128]{2,1,0:T(8,128)S(1)} %get-tuple-element.86), channel_id=1, source_target_pairs={{0,4},{1,5},{2,6},{3,7},{4,0},{5,1},{6,2},{7,3},{8,12},{9,13},{10,... | collective-permute-start | bytes 491528 | tf_op jit(solution)/shard_map/cond/branch_3_fun/ppermute | solution.py:445
  15.3 2.1 %collective-permute-start.26 = (f32[40,8,128]{2,1,0:T(8,128)S(1)}, f32[40,8,128]{2,1,0:T(8,128)S(1)}, u32[]{:S(2)}, u32[]{:S(2)}) collective-permute-start(f32[40,8,128]{2,1,0:T(8,128)S(1)} %get-tuple-element.87), channel_id=1, source_target_pairs={{0,28},{1,29},{2,30},{3,31},{4,8},{5,9},{6,10},{7,11},{8,4},{9,5},... | collective-permute-start | bytes 491528 | tf_op jit(solution)/shard_map/cond/branch_3_fun/ppermute | solution.py:446
  17.4 0.1 join.7.own
  17.5 0.1 collective-permute-start.22
  17.6 0.7 %collective-permute-start.23 = (f32[4,16,128]{2,1,0:T(8,128)S(1)}, f32[4,16,128]{2,1,0:T(8,128)S(1)}, u32[]{:S(2)}, u32[]{:S(2)}) collective-permute-start(f32[4,16,128]{2,1,0:T(8,128)S(1)} %join.7.own), channel_id=1, source_target_pairs={{0,28},{1,29},{2,30},{3,31},{4,8},{5,9},{6,10},{7,11},{8,4},{9,5},... | collective-permute-start | bytes 98312 | tf_op jit(solution)/shard_map/cond/branch_3_fun/ppermute | solution.py:440
  18.3 0.5 %collective-permute-done.22.first = f32[4,16,128]{2,1,0:T(8,128)S(1)} collective-permute-done((f32[4,16,128]{2,1,0:T(8,128)S(1)}, f32[4,16,128]{2,1,0:T(8,128)S(1)}, u32[]{:S(2)}, u32[]{:S(2)}) %collective-permute-start.22) | collective-permute-done | bytes 32800 | tf_op jit(solution)/shard_map/cond/branch_3_fun/ppermute | solution.py:439
  18.8 4.3 %collective-permute-done.23.second = f32[4,16,128]{2,1,0:T(8,128)S(1)} collective-permute-done((f32[4,16,128]{2,1,0:T(8,128)S(1)}, f32[4,16,128]{2,1,0:T(8,128)S(1)}, u32[]{:S(2)}, u32[]{:S(2)}) %collective-permute-start.23) | collective-permute-done | bytes 32800 | tf_op jit(solution)/shard_map/cond/branch_3_fun/ppermute | solution.py:440
  23.1 1.1 %far.7 = f32[2,16,128]{2,1,0:T(8,128)S(1)} custom-call(s32[2]{0:T(128)S(1)} %get-tuple-element.81.offsets, f32[4,16,128]{2,1,0:T(8,128)S(1)} %join.7.own, f32[4,16,128]{2,1,0:T(8,128)S(1)} %collective-permute-done.22.first, f32[4,16,128]{2,1,0:T(8,128)S(1)} %collective-permute-done.23.second), custom_call_target="tpu_custom_call" | custom-call | bytes 262144 | tf_op jit(solution)/shard_map/cond/branch_3_fun/far/pallas_call | solution.py:385
  24.2 1.2 %collective-permute-start.27 = (f32[2,16,128]{2,1,0:T(8,128)S(1)}, f32[2,16,128]{2,1,0:T(8,128)S(1)}, u32[]{:S(2)}, u32[]{:S(2)}) collective-permute-start(f32[2,16,128]{2,1,0:T(8,128)S(1)} %far.7), channel_id=1, source_target_pairs={{0,16},{1,17},{2,18},{3,19},{4,20},{5,21},{6,22},{7,23},{8,24},{9,... | collective-permute-start | bytes 49160 | tf_op jit(solution)/shard_map/cond/branch_3_fun/ppermute | solution.py:459
  25.4 0.0 collective-permute-done.25.first_bulk
  25.4 0.0 collective-permute-done.26.second_bulk
  25.4 3.1 %first_section.7 = (f32[8,4,32,128]{3,2,1,0:T(8,128)S(1)}, f32[8,16,128]{2,1,0:T(8,128)S(1)}) custom-call(s32[2]{0:T(128)S(1)} %get-tuple-element.81.offsets, f32[8,4,16,128]{3,2,1,0:T(8,128)S(1)} %get-tuple-element.80.state, f32[4,16,128]{2,1,0:T(8,128)S(1)} %join.7.own, f32[4,16,128]{2,1,0:T(8,128)S(1)} %collective-permute-done.22.first, ...), custom_call_target="tpu_custom_call" | custom-call | flops 8388608 | bytes 262144 | tf_op jit(solution)/shard_map/cond/branch_3_fun/first_section/pallas_call | solution.py:385
  28.4 0.0 collective-permute-done.27.packed
  28.4 1.0 %second_section.7 = f32[8,4,16,128]{3,2,1,0:T(8,128)S(1)} custom-call(f32[8,4,16,128]{3,2,1,0:T(8,128)S(1)} %get-tuple-element.80.state, f32[8,4,32,128]{3,2,1,0:T(8,128)S(1)} %get-tuple-element.88.section, f32[8,16,128]{2,1,0:T(8,128)S(1)} %get-tuple-element.89.strips, f32[2,16,128]{2,1,0:T(8,128)S(1)} %collective-permute-done.27.packed), custom_call_target="tpu_custom_call" | custom-call | flops 4194304 | bytes 262144 | tf_op jit(solution)/shard_map/cond/branch_3_fun/second_section/pallas_call | solution.py:385
  29.6 0.0 copy-start.4
  29.7 0.7 %copy-done.4 = f32[8,4,16,128]{3,2,1,0:T(8,128)} copy-done((f32[8,4,16,128]{3,2,1,0:T(8,128)}, f32[8,4,16,128]{3,2,1,0:T(8,128)S(1)}, u32[]{:S(2)}) %copy-start.4) | copy-done | bytes 262168
  (5 shorter events, 0.0 us)
Async XLA Ops:
  0.0 0.9 %copy-start = (f32[3,4,16,128]{3,2,1,0:T(8,128)S(1)}, f32[3,4,16,128]{3,2,1,0:T(8,128)}, u32[]{:S(2)}) copy-start(f32[3,4,16,128]{3,2,1,0:T(8,128)} %momentum.1) | copy-start | bytes 294916
  0.9 0.9 %copy-start.1 = (f32[3,4,16,128]{3,2,1,0:T(8,128)S(1)}, f32[3,4,16,128]{3,2,1,0:T(8,128)}, u32[]{:S(2)}) copy-start(f32[3,4,16,128]{3,2,1,0:T(8,128)} %magnetic.1) | copy-start | bytes 294916
  1.8 0.8 %copy-start.2 = (f32[4,16,128]{2,1,0:T(8,128)S(1)}, f32[4,16,128]{2,1,0:T(8,128)}, u32[]{:S(2)}) copy-start(f32[4,16,128]{2,1,0:T(8,128)} %density.1) | copy-start | bytes 98308
  2.5 0.8 %copy-start.3 = (f32[4,16,128]{2,1,0:T(8,128)S(1)}, f32[4,16,128]{2,1,0:T(8,128)}, u32[]{:S(2)}) copy-start(f32[4,16,128]{2,1,0:T(8,128)} %tracer.1) | copy-start | bytes 98308
  3.6 0.7 %copy-start.5 = (s32[2]{0:T(128)S(1)}, s32[2]{0:T(128)}, u32[]{:S(2)}) copy-start(s32[2]{0:T(128)} %param.14) | copy-start | bytes 28
  3.6 0.7 %copy-start.6 = (s32[2]{0:T(128)S(1)}, s32[2]{0:T(128)}, u32[]{:S(2)}) copy-start(s32[2]{0:T(128)} %constant.11.clone) | copy-start | bytes 28
  6.4 6.0 %collective-permute-start.21 = (f32[2,16,128]{2,1,0:T(8,128)S(1)}, f32[2,16,128]{2,1,0:T(8,128)S(1)}, u32[]{:S(2)}, u32[]{:S(2)}) collective-permute-start(f32[2,16,128]{2,1,0:T(8,128)S(1)} %get-tuple-element.83), channel_id=1, source_target_pairs={{0,7},{1,2},{2,1},{3,28},{4,11},{5,6},{6,5},{7,0},{8,15},{9,10},{1... | collective-permute-start | bytes 49160 | tf_op jit(solution)/shard_map/cond/branch_3_fun/ppermute | solution.py:436
  11.0 3.8 %collective-permute-start.24 = (f32[2,16,128]{2,1,0:T(8,128)S(1)}, f32[2,16,128]{2,1,0:T(8,128)S(1)}, u32[]{:S(2)}, u32[]{:S(2)}) collective-permute-start(f32[2,16,128]{2,1,0:T(8,128)S(1)} %get-tuple-element.84), channel_id=1, source_target_pairs={{0,1},{1,0},{2,3},{3,2},{4,5},{5,4},{6,7},{7,6},{8,9},{9,8},{10,11... | collective-permute-start | bytes 49160 | tf_op jit(solution)/shard_map/cond/branch_3_fun/ppermute | solution.py:437
  14.8 10.5 %collective-permute-start.25 = (f32[40,8,128]{2,1,0:T(8,128)S(1)}, f32[40,8,128]{2,1,0:T(8,128)S(1)}, u32[]{:S(2)}, u32[]{:S(2)}) collective-permute-start(f32[40,8,128]{2,1,0:T(8,128)S(1)} %get-tuple-element.86), channel_id=1, source_target_pairs={{0,4},{1,5},{2,6},{3,7},{4,0},{5,1},{6,2},{7,3},{8,12},{9,13},{10,... | collective-permute-start | bytes 491528 | tf_op jit(solution)/shard_map/cond/branch_3_fun/ppermute | solution.py:445
  15.3 10.0 %collective-permute-start.26 = (f32[40,8,128]{2,1,0:T(8,128)S(1)}, f32[40,8,128]{2,1,0:T(8,128)S(1)}, u32[]{:S(2)}, u32[]{:S(2)}) collective-permute-start(f32[40,8,128]{2,1,0:T(8,128)S(1)} %get-tuple-element.87), channel_id=1, source_target_pairs={{0,28},{1,29},{2,30},{3,31},{4,8},{5,9},{6,10},{7,11},{8,4},{9,5},... | collective-permute-start | bytes 491528 | tf_op jit(solution)/shard_map/cond/branch_3_fun/ppermute | solution.py:446
  17.5 1.3 %collective-permute-start.22 = (f32[4,16,128]{2,1,0:T(8,128)S(1)}, f32[4,16,128]{2,1,0:T(8,128)S(1)}, u32[]{:S(2)}, u32[]{:S(2)}) collective-permute-start(f32[4,16,128]{2,1,0:T(8,128)S(1)} %join.7.own), channel_id=1, source_target_pairs={{0,4},{1,5},{2,6},{3,7},{4,0},{5,1},{6,2},{7,3},{8,12},{9,13},{10,... | collective-permute-start | bytes 98312 | tf_op jit(solution)/shard_map/cond/branch_3_fun/ppermute | solution.py:439
  17.6 5.5 %collective-permute-start.23 = (f32[4,16,128]{2,1,0:T(8,128)S(1)}, f32[4,16,128]{2,1,0:T(8,128)S(1)}, u32[]{:S(2)}, u32[]{:S(2)}) collective-permute-start(f32[4,16,128]{2,1,0:T(8,128)S(1)} %join.7.own), channel_id=1, source_target_pairs={{0,28},{1,29},{2,30},{3,31},{4,8},{5,9},{6,10},{7,11},{8,4},{9,5},... | collective-permute-start | bytes 98312 | tf_op jit(solution)/shard_map/cond/branch_3_fun/ppermute | solution.py:440
  24.2 4.2 %collective-permute-start.27 = (f32[2,16,128]{2,1,0:T(8,128)S(1)}, f32[2,16,128]{2,1,0:T(8,128)S(1)}, u32[]{:S(2)}, u32[]{:S(2)}) collective-permute-start(f32[2,16,128]{2,1,0:T(8,128)S(1)} %far.7), channel_id=1, source_target_pairs={{0,16},{1,17},{2,18},{3,19},{4,20},{5,21},{6,22},{7,23},{8,24},{9,... | collective-permute-start | bytes 49160 | tf_op jit(solution)/shard_map/cond/branch_3_fun/ppermute | solution.py:459
  29.6 0.7 %copy-start.4 = (f32[8,4,16,128]{3,2,1,0:T(8,128)}, f32[8,4,16,128]{3,2,1,0:T(8,128)S(1)}, u32[]{:S(2)}) copy-start(f32[8,4,16,128]{3,2,1,0:T(8,128)S(1)} %get-tuple-element.153) | copy-start | bytes 786436

commit v2 on v1

v2 whole, which is shorter than its diff:
```python
import functools

import jax
import jax.numpy as jnp
from jax import lax
from jax.experimental import pallas as pl
from jax.experimental.pallas import tpu as pltpu
from jax.sharding import PartitionSpec as P

time_step = 0.025
viscosity = 0.5
sound_squared = 1.0
shear_speed = 1.0
frac_weight = 0.375
stencil = ((1, 45.0 / 60.0), (2, -9.0 / 60.0), (3, 1.0 / 60.0))
REACH = 3
FIELDS = 8
SUB = 8
RIGHT = 16
PACK = 8


def struct(*shape):
    return jax.ShapeDtypeStruct(shape, jnp.float32)


def lanes_of(shape):
    return lax.broadcasted_iota(jnp.int32, shape, len(shape) - 1)


def move(values, by):
    count = values.shape[-1]
    if isinstance(by, int):
        by = by % count
        return values if by == 0 else pltpu.roll(values, by, values.ndim - 1)
    return pltpu.roll(values, lax.rem(by + count, count), values.ndim - 1)


def primitives(cells):
    inverse = 1.0 / cells[0]
    velocity = [cells[1 + i] * inverse for i in range(3)]
    squares = cells[4] * cells[4] + cells[5] * cells[5] + cells[6] * cells[6]
    return velocity, sound_squared * cells[0] + 0.5 * squares


def flux(cells, velocity, pressure, direction):
    speed, normal = velocity[direction], cells[4 + direction]
    result = [cells[1 + direction]]
    for i in range(3):
        term = cells[1 + i] * speed - cells[4 + i] * normal
        result.append(term + pressure if i == direction else term)
    for i in range(3):
        result.append(None if i == direction else speed * cells[4 + i] - normal * velocity[i])
    result.append(cells[7] * speed)
    return result


def along_lanes(values, flows, lane, halo_values=None, halo_flows=None):
    count = values.shape[-1]

    def ends(array, halo, width):
        if halo is None:
            return array, array
        return jnp.where(lane < width, halo, array), jnp.where(lane >= count - width, halo, array)

    above, below = ends(values, halo_values, 1)
    up, down = viscosity * above, viscosity * below
    if flows is None:
        return move(up, -1) + move(down, 1)
    total = None
    for distance, weight in stencil:
        above, below = ends(flows, halo_flows, distance)
        plus, minus = -weight * above, weight * below
        if distance == 1:
            plus, minus = plus + up, minus + down
        pair = move(plus, -distance) + move(minus, distance)
        total = pair if total is None else total + pair
    return total


def layer_weights(layers):
    folded = {}
    for distance, weight in stencil:
        for signed, share in ((distance, weight), (-distance, -weight)):
            folded[signed % layers] = folded.get(signed % layers, 0.0) + share
    return {distance: weight for distance, weight in folded.items() if weight != 0.0 and distance != 0}


def strip_section(cells, flows_ref, cells_ref, layers):
    rows, count = cells[0].shape
    slot = count // layers
    velocity, pressure = primitives(cells)
    flow_x, flow_y, flow_z = (flux(cells, velocity, pressure, d) for d in range(3))
    weights = layer_weights(layers)
    result = []
    for f in range(FIELDS):
        cells_ref[f, SUB : SUB + rows] = cells[f]
        if flow_y[f] is not None:
            flows_ref[f, SUB : SUB + rows] = flow_y[f]
    for f in range(FIELDS):
        total = along_lanes(cells[f], flow_x[f], None)
        total = total + viscosity * (move(cells[f], slot) + move(cells[f], -slot))
        if flow_z[f] is not None:
            for distance, weight in weights.items():
                total = total - weight * move(flow_z[f], -distance * slot)
        total = total + viscosity * (cells_ref[f, SUB - 1 : SUB - 1 + rows] + cells_ref[f, SUB + 1 : SUB + 1 + rows])
        if flow_y[f] is not None:
            for distance, weight in stencil:
                total = total - weight * (
                    flows_ref[f, SUB + distance : SUB + distance + rows]
                    - flows_ref[f, SUB - distance : SUB - distance + rows]
                )
        total = total - 6.0 * viscosity * cells[f]
        result.append(cells[f] + time_step * total)
    return result


def sheared(lead, trail, inner):
    first = jnp.where(inner, 1.0 - frac_weight, frac_weight)
    jump = jnp.where(inner, shear_speed, -shear_speed)
    ghosts = [first * a + (1.0 - first) * b for a, b in zip(lead, trail)]
    ghosts[2] = ghosts[2] + jump * ghosts[0]
    return ghosts


def split_pairs(pairs):
    return [pairs[f // 2] if f % 2 == 0 else move(pairs[f // 2], -RIGHT) for f in range(FIELDS)]


def fill_window(window_ref, own_ref, first_ref, second_ref, even):
    tiles, rows, _ = own_ref.shape
    parts = rows // SUB
    for t in range(tiles):
        window_ref[t, SUB + rows : SUB + 2 * rows] = own_ref[t]
        for i in range(parts):
            before, after = neighbours(first_ref[t * parts + i], second_ref[t * parts + i], even)
            window_ref[t, SUB + i * SUB : SUB + (i + 1) * SUB] = before
            window_ref[t, SUB + 2 * rows + i * SUB : SUB + 2 * rows + (i + 1) * SUB] = after


def neighbours(first, second, even):
    return jnp.where(even, second, first), jnp.where(even, first, second)


def axis_place(axis):
    place = lax.axis_index(axis)
    return lax.rem(place, 2), place == 0, place == lax.axis_size(axis) - 1


def rows_for(rows):
    odd, _, _ = axis_place("az")
    return pl.multiple_of((1 - odd) * (rows - SUB), SUB), pl.multiple_of(odd * (rows - SUB), SUB)


def edges_kernel(density, momentum, magnetic, tracer, offsets, state, near, far, pairs, index, shifts, *rest):
    *bulks, held, sems = rest
    layers, rows, cols = density.shape
    slot = cols // layers
    parts = (
        (density, state.at[0]),
        (momentum, state.at[1:4]),
        (magnetic, state.at[4:7]),
        (tracer, state.at[7]),
        (offsets, held),
    )
    copies = [pltpu.make_async_copy(source, target, sems.at[i]) for i, (source, target) in enumerate(parts)]
    for copy in copies:
        copy.start()
    odd, _, last = axis_place("rad")
    lane = lanes_of((rows, cols))
    width = 2 * REACH
    near_parts, far_parts = [jnp.zeros((rows, cols), jnp.float32)] * 2, [jnp.zeros((rows, cols), jnp.float32)] * 2
    pair_parts = [jnp.zeros((rows, cols), jnp.float32)] * 4
    shift_pair = jnp.where(last, REACH, width)
    for f in range(FIELDS):
        if f in (0, 1, 4, 7):
            copies[(0, 1, 4, 7).index(f)].wait()
        for z in range(layers):
            plane = state[f, z]
            start = z * slot + (f % 4) * PACK
            inside = (lane >= start) & (lane < start + PACK)
            left, right = move(plane, start), move(plane, start + width)
            near_parts[f // 4] = jnp.where(inside, jnp.where(odd == 1, right, left), near_parts[f // 4])
            far_parts[f // 4] = jnp.where(inside, jnp.where(odd == 1, left, right), far_parts[f // 4])
            start = z * slot + (f % 2) * RIGHT
            begin = start + jnp.where(last, 0, width)
            inside = (lane >= begin) & (lane < begin + REACH)
            pair_parts[f // 2] = jnp.where(inside, move(plane, start + shift_pair), pair_parts[f // 2])
    for part in range(2):
        near[part], far[part] = near_parts[part], far_parts[part]
    for part in range(2, far.shape[0]):
        far[part] = jnp.zeros((rows, cols), jnp.float32)
    for part in range(2, near.shape[0]):
        near[part] = jnp.zeros((rows, cols), jnp.float32)
    for part in range(4):
        pairs[part] = pair_parts[part]
    odd_az, _, _ = axis_place("az")
    for f in range(FIELDS):
        for z in range(layers):
            head, tail = state[f, z, :width, :], state[f, z, rows - width :, :]
            place = slice((f * layers + z) * width, (f * layers + z + 1) * width)
            bulks[0][place, :] = jnp.where(odd_az == 1, head, tail)
            bulks[1][place, :] = jnp.where(odd_az == 1, tail, head)
    copies[4].wait()
    half = rows * lax.axis_size("az") // 2
    for i in range(2):
        shifts[i : i + 1, :] = jnp.full((1, cols), held[i])
    index[...] = jnp.full((1,), jnp.where(held[0] > rows - 4, 2, 0) + jnp.where(held[1] > rows - 4 + half, 1, 0))


def join_kernel(pairs, near, far, own, halo, first, second):
    odd, _, last = axis_place("rad")
    tiles, rows, cols = pairs.shape
    slot = 2 * RIGHT
    lane = lax.rem(lanes_of((rows, cols)), slot)
    offset = jnp.where(last, REACH, 0)
    parts = rows // SUB
    starts = rows_for(rows)
    for part in range(tiles):
        total = pairs[part]
        for f in (2 * part, 2 * part + 1):
            begin = (f % 2) * RIGHT + offset
            inside = (lane >= begin) & (lane < begin + 2 * REACH)
            total = jnp.where(inside, move(near[f // 4], begin - (f % 4) * PACK), total)
        own[part] = total
        for i in range(parts):
            first[part * parts + i] = second[part * parts + i] = total[i * SUB : (i + 1) * SUB]
    for f in range(FIELDS):
        a, b = far[f // 4], near[f // 4]
        left, right = jnp.where(odd == 1, a, b), jnp.where(odd == 1, b, a)
        left, right = move(left, -(f % 4) * PACK), move(right, RIGHT + REACH - (f % 4) * PACK)
        halo[f] = jnp.where(
            lane < 2 * REACH,
            left,
            jnp.where((lane >= RIGHT + REACH) & (lane < RIGHT + 3 * REACH), right, 0.0),
        )
        for out, start in zip((first, second), starts):
            out[tiles * parts + f] = halo[f, pl.ds(start, SUB), :]


def far_kernel(offsets, own, first, second, packed, window, flows_ref, cells_ref, *, turn, wrap):
    odd_az, _, _ = axis_place("az")
    _, _, last = axis_place("rad")
    tiles, rows, cols = own.shape
    layers = cols // (2 * RIGHT)
    total_rows = rows * lax.axis_size("az")
    fill_window(window, own, first, second, odd_az == 0)
    shift, turned = offsets[0, 0], offsets[1, 0] - total_rows // 2
    height = rows + SUB
    base = SUB + rows
    begin = jnp.where(last, base - REACH - 1 - turned + wrap * rows, base - REACH + turned - wrap * rows)
    edge = jnp.where(
        last, base - REACH - 1 - turned + turn * rows + shift, base - REACH + turned - turn * rows - shift - 1
    )
    cells = split_pairs([window[t, pl.ds(begin, height), :] for t in range(tiles)])
    lead = split_pairs([window[t, pl.ds(edge, height), :] for t in range(tiles)])
    trail = split_pairs([window[t, pl.ds(edge + 1, height), :] for t in range(tiles)])
    lane = lax.rem(lanes_of((height, cols)), 2 * RIGHT)
    ghost_start = jnp.where(last, 0, 2 * REACH)
    ghost_lane = (lane >= ghost_start) & (lane < ghost_start + REACH)
    ghosts = sheared(lead, trail, last)
    cells = [jnp.where(ghost_lane, g, c) for g, c in zip(ghosts, cells)]
    section = strip_section(cells, flows_ref, cells_ref, layers)
    lead, trail = [], []
    for f in range(FIELDS):
        flows_ref[f, SUB : SUB + height] = section[f]
        lead.append(flows_ref[f, SUB + REACH : SUB + REACH + rows])
        trail.append(flows_ref[f, SUB + REACH + 1 : SUB + REACH + 1 + rows])
    ghosts = sheared(lead, trail, jnp.logical_not(last))
    lane = lax.rem(lanes_of((rows, cols)), 2 * RIGHT)
    for part in range(2):
        total = jnp.zeros((rows, cols), jnp.float32)
        for i in range(4):
            inside = (lane >= i * PACK) & (lane < (i + 1) * PACK)
            total = jnp.where(inside, move(ghosts[4 * part + i], i * PACK - REACH), total)
        packed[part] = total


def section_tiles(cells_ref, flow_y, flow_z, partial, tiles, emit):
    _, layers, rows, cols = cells_ref.shape
    lane = lanes_of((SUB, cols))
    weights = layer_weights(layers)
    for z in range(layers):
        for t in range(rows // SUB):
            span = pl.ds(t * SUB, SUB)
            cells = [cells_ref[f, z, span, :] for f in range(FIELDS)]
            velocity, pressure = primitives(cells)
            flows = flux(cells, velocity, pressure, 1)
            for f in range(FIELDS):
                if flows[f] is not None:
                    flow_y[f, z, span, :] = flows[f]
            if t not in tiles:
                continue
            flows = flux(cells, velocity, pressure, 2)
            for f in range(FIELDS):
                if flows[f] is not None:
                    flow_z[f, z, span, :] = flows[f]
            flows = flux(cells, velocity, pressure, 0)
            for f in range(FIELDS):
                partial[f, z, span, :] = along_lanes(cells[f], flows[f], lane, 0.0, 0.0)
    for z in range(layers):
        for t in tiles:
            start = t * SUB
            for f in range(FIELDS):

                def near(ref, layer, shift, f=f, start=start):
                    return ref[f, layer, pl.ds(start + shift, SUB), :]

                cells = near(cells_ref, z, 0)
                total = partial[f, z, pl.ds(start, SUB), :]
                around = near(cells_ref, z, 1) + near(cells_ref, z, -1)
                around = around + near(cells_ref, (z + 1) % layers, 0) + near(cells_ref, (z - 1) % layers, 0)
                total = total + viscosity * (around - 6.0 * cells)
                if f != 5:
                    for distance, weight in stencil:
                        total = total - weight * (near(flow_y, z, distance) - near(flow_y, z, -distance))
                if f != 6:
                    for distance, weight in weights.items():
                        total = total - weight * near(flow_z, (z + distance) % layers, 0)
                emit(f, z, t, cells + time_step * total)


def end_terms(halo, layers):
    lane = lax.rem(lanes_of(halo[0].shape), halo[0].shape[-1] // layers)
    low, high = (lane >= REACH) & (lane < 2 * REACH), (lane >= 2 * REACH) & (lane < 3 * REACH)
    velocity, pressure = primitives(halo)
    flows = flux(halo, velocity, pressure, 0)
    result = []
    for f in range(FIELDS):
        up, down = move(halo[f], 1), move(halo[f], -1)
        from_low = jnp.where(lane < 2 * REACH + 1, viscosity * up, 0.0)
        from_high = jnp.where(lane >= 2 * REACH - 1, viscosity * down, 0.0)
        if flows[f] is not None:
            for distance, weight in stencil:
                from_low = from_low + jnp.where(lane < 2 * REACH + distance, weight * move(flows[f], distance), 0.0)
                from_high = from_high - jnp.where(lane >= 2 * REACH - distance, weight * move(flows[f], -distance), 0.0)
        result.append(jnp.where(high, from_low, jnp.where(low, from_high, 0.0)))
    return result


def to_plane(strip, z, layers):
    return move(strip, -(z * (strip.shape[-1] // layers) + 2 * REACH))


def ends_strip(left, right, lane):
    return jnp.where(lane < 2 * REACH, left, right)


def first_kernel(state, first, second, section, cells_ref, flow_y, flow_z, partial):
    odd_az, _, _ = axis_place("az")
    _, layers, rows, _ = state.shape
    even = odd_az == 0
    width = 2 * REACH
    for f in range(FIELDS):
        for z in range(layers):
            place = slice((f * layers + z) * width, (f * layers + z + 1) * width)
            before, after = neighbours(first[place, :], second[place, :], even)
            cells_ref[f, z, 2 * SUB - width : 2 * SUB, :] = before
            cells_ref[f, z, 2 * SUB : 2 * SUB + rows, :] = state[f, z]
            cells_ref[f, z, 2 * SUB + rows : 2 * SUB + rows + width, :] = after

    def emit(f, z, t, value):
        section[f, z, (t - 1) * SUB : t * SUB, :] = value

    section_tiles(cells_ref, flow_y, flow_z, partial, range(1, 3 + rows // SUB), emit)


def ends_kernel(shifts, state, own, first, second, halo, partial, section, strips, window, flows_ref, strip_ref, *, wrap):
    odd_az, _, _ = axis_place("az")
    _, begins, last = axis_place("rad")
    _, layers, rows, cols = state.shape
    slot = cols // layers
    height = rows + 2 * SUB
    even = odd_az == 0
    fill_window(window, own, first, second, even)
    shift = shifts[0, 0]
    begin = jnp.where(last, rows - 1 - shift + wrap * rows, rows + shift - wrap * rows)
    lead = split_pairs([window[t, pl.ds(begin, height), :] for t in range(own.shape[0])])
    trail = split_pairs([window[t, pl.ds(begin + 1, height), :] for t in range(own.shape[0])])
    ghosts = sheared(lead, trail, begins)
    lane = lax.rem(lanes_of((height, cols)), slot)
    whole = lanes_of((rows, cols))
    own_lane = ((lane >= 2 * REACH) & (lane < 3 * REACH)) | ((lane >= RIGHT) & (lane < RIGHT + REACH))
    blank = jnp.zeros((SUB, cols), jnp.float32)
    strip_cells, beyond = [], []
    for f in range(FIELDS):
        corner = first.shape[0] - FIELDS + f
        before, after = neighbours(first[corner], second[corner], even)
        strip = jnp.concatenate([before, halo[f], after], axis=0)
        own_part = jnp.zeros((rows, cols), jnp.float32)
        for z in range(layers):
            low = z * slot + 2 * REACH
            own_part = jnp.where((whole >= low) & (whole < low + REACH), move(state[f, z], low), own_part)
            low = z * slot + RIGHT
            own_part = jnp.where((whole >= low) & (whole < low + REACH), move(state[f, z], low + REACH), own_part)
        own_part = jnp.concatenate([blank, own_part, blank], axis=0)
        strip_cells.append(jnp.where(own_lane, own_part, strip))
        right = move(strip, 2 * REACH - RIGHT - REACH)
        left = jnp.where(begins, ghosts[f], strip)
        right = jnp.where(last, move(ghosts[f], REACH), right)
        beyond.append(ends_strip(left, right, lane))
    terms = end_terms(beyond, layers)
    column = lanes_of((height, cols))
    ends = (column < REACH) | (column >= cols - REACH)
    for f in range(FIELDS):
        for z in range(layers):
            added = jnp.where(ends, time_step * to_plane(terms[f], z, layers), 0.0)
            section[f, z] = partial[f, z] + added
    done = strip_section(strip_cells, flows_ref, strip_ref, layers)
    for f in range(FIELDS):
        right = move(done[f], 2 * REACH - RIGHT - REACH)
        strips[f] = ends_strip(done[f], right, lane)[SUB : SUB + rows]


def second_kernel(state, section, result, flow_y, flow_z, partial):
    _, _, rows, _ = state.shape

    def emit(f, z, t, value):
        rows_of = slice((t - 1) * SUB, t * SUB)
        result[f, z, rows_of, :] = 0.5 * state[f, z, rows_of, :] + 0.5 * value

    section_tiles(section, flow_y, flow_z, partial, range(1, 1 + rows // SUB), emit)


def last_kernel(partial, strips, packed, result):
    _, begins, last = axis_place("rad")
    _, layers, rows, cols = partial.shape
    lane = lax.rem(lanes_of((rows, cols)), cols // layers)
    halo = []
    for f in range(FIELDS):
        ghosts = packed[f // 4]
        left = jnp.where(begins, move(ghosts, REACH - (f % 4) * PACK), strips[f])
        right = jnp.where(last, move(ghosts, 2 * REACH - (f % 4) * PACK), strips[f])
        halo.append(ends_strip(left, right, lane))
    terms = end_terms(halo, layers)
    column = lanes_of((rows, cols))
    ends = (column < REACH) | (column >= cols - REACH)
    for f in range(FIELDS):
        for z in range(layers):
            added = jnp.where(ends, 0.5 * time_step * to_plane(terms[f], z, layers), 0.0)
            result[f, z] = partial[f, z] + added


VMEM = pl.BlockSpec(memory_space=pltpu.VMEM)
SMEM = pl.BlockSpec(memory_space=pltpu.SMEM)
HBM = pl.BlockSpec(memory_space=pltpu.HBM)


BIG = 63 * 2**20


def call(kernel, name, outs, *args, scratch=(), flops=0, smem=0, hbm=0, sems=0, out_spec=VMEM, limit=24 * 2**20, cost=2**18):
    many = isinstance(outs, list)
    scratch_shapes = [pltpu.VMEM(shape, jnp.float32) for shape in scratch]
    if sems:
        scratch_shapes.append(pltpu.SemaphoreType.DMA((sems,)))
    return pl.pallas_call(
        kernel,
        name=name,
        out_shape=outs,
        in_specs=[SMEM] * smem + [HBM] * hbm + [VMEM] * (len(args) - smem - hbm),
        out_specs=[out_spec] * len(outs) if many else out_spec,
        scratch_shapes=scratch_shapes,
        compiler_params=pltpu.CompilerParams(vmem_limit_bytes=limit),
        cost_estimate=pl.CostEstimate(flops=flops, bytes_accessed=cost, transcendentals=0),
    )(*args)


def routes(az_count, rad_count, wrap, turn):
    def listed(target):
        pairs = []
        for a in range(az_count):
            for r in range(rad_count):
                to_a, to_r = target(a, r)
                pairs.append((a * rad_count + r, (to_a % az_count) * rad_count + to_r))
        return pairs

    end = rad_count - 1

    def near(a, r):
        if r == 0:
            return a + wrap, end
        if r == end:
            return a - wrap, 0
        return a, r + 1 if r % 2 else r - 1

    def half_turn(a, r):
        extra = -turn if r == 0 else turn if r == end else 0
        return a + az_count // 2 + extra, r

    return (
        listed(near),
        listed(lambda a, r: (a, r ^ 1)),
        listed(lambda a, r: (a ^ 1, r)),
        listed(lambda a, r: (((a + 1) ^ 1) - 1, r)),
        listed(half_turn),
    )


def exchange_and_step(wrap, turned_wrap, shifts, state, near, far, pairs, *bulks):
    _, layers, rows, cols = state.shape
    turn = turned_wrap - wrap
    near_route, far_route, first_route, second_route, turn_route = routes(
        lax.axis_size("az"), lax.axis_size("rad"), wrap, turn
    )
    axes = ("az", "rad")
    far_in = lax.ppermute(far, axes, far_route)
    near_in = lax.ppermute(near, axes, near_route)
    bulks = [lax.ppermute(part, axes, (first_route, second_route)[i]) for i, part in enumerate(bulks)]
    parcel = struct(4 * rows // SUB + FIELDS, SUB, cols)
    own, halo, for_first, for_second = call(
        join_kernel,
        "join",
        [struct(4, rows, cols), struct(FIELDS, rows, cols), parcel, parcel],
        pairs,
        near_in,
        far_in,
    )
    first = lax.ppermute(for_first, axes, first_route)
    second = lax.ppermute(for_second, axes, second_route)
    height = rows + 2 * SUB
    padded = (FIELDS, layers, height + 2 * SUB, cols)
    partial = call(
        first_kernel,
        "first_section",
        struct(FIELDS, layers, height, cols),
        state,
        *bulks,
        scratch=[padded] * 4,
    )
    window = (4, 3 * rows + 2 * SUB, cols)
    packed = call(
        functools.partial(far_kernel, turn=turn, wrap=turned_wrap),
        "far",
        struct(2, rows, cols),
        shifts,
        own,
        first,
        second,
        scratch=[window] + [(FIELDS, rows + 3 * SUB, cols)] * 2,
    )
    packed = lax.ppermute(packed, axes, turn_route)
    section, strips = call(
        functools.partial(ends_kernel, wrap=wrap),
        "first_ends",
        [struct(FIELDS, layers, height, cols), struct(FIELDS, rows, cols)],
        shifts,
        state,
        own,
        first,
        second,
        halo,
        partial,
        scratch=[window] + [(FIELDS, height + 2 * SUB, cols)] * 2,
    )
    partial = call(
        second_kernel,
        "second_section",
        struct(FIELDS, layers, rows, cols),
        state,
        section,
        scratch=[(FIELDS, layers, height, cols)] * 3,
    )
    return call(last_kernel, "second_ends", struct(FIELDS, layers, rows, cols), partial, strips, packed)


def shards(density, momentum, magnetic, tracer, offsets):
    layers, rows, cols = density.shape
    state, near, far, pairs, index, shifts, *bulks = pl.pallas_call(
        edges_kernel,
        name="edges",
        out_shape=[
            struct(FIELDS, layers, rows, cols),
            struct(3, rows, cols),
            struct(4, rows, cols),
            struct(4, rows, cols),
            jax.ShapeDtypeStruct((1,), jnp.int32),
            jax.ShapeDtypeStruct((SUB, cols), jnp.int32),
        ]
        + [struct(FIELDS * layers * 2 * REACH, cols)] * 2,
        in_specs=[HBM] * 5,
        out_specs=[VMEM] * 8,
        scratch_shapes=[pltpu.SMEM((2,), jnp.int32), pltpu.SemaphoreType.DMA((5,))],
        compiler_params=pltpu.CompilerParams(vmem_limit_bytes=BIG),
    )(density, momentum, magnetic, tracer, offsets)
    branches = [
        functools.partial(exchange_and_step, wrap, turned_wrap) for wrap in range(2) for turned_wrap in range(2)
    ]
    return lax.switch(index[0], branches, shifts, state, near, far, pairs, *bulks)


def solution(mesh):
    placed = (
        P(None, "az", "rad"),
        P(None, None, "az", "rad"),
        P(None, None, "az", "rad"),
        P(None, "az", "rad"),
        P(),
    )
    return jax.shard_map(
        shards, mesh=mesh, in_specs=placed, out_specs=P(None, None, "az", "rad"), check_vma=False
    )
```

time: 30.5 us -> 22.6 us (0.74)
  waiting for transfers between devices: 8.5 us -> 2.79 us
  local copies, waits for them, and re-layouts: 5.24 us -> 0.7 us
  starting transfers between devices: 9.18 us -> 12.6 us
  between operations: 1.34 us -> 0.67 us
    unnamed x14 -> x2, local copies, waits for them, and re-layouts: 4.65 us -> 0.7 us
    ppermute x1, starting transfers between devices: 0.11 us -> 3.09 us  [exchange_and_step(): far_in = lax.ppermute(far, axes, far_route)]
    ppermute x4, waiting for transfers between devices: 4.86 us -> 2.19 us  [the longest x1 2.19 us: exchange_and_step(): second = lax.ppermute(for_second, axes, second_route)]
    ppermute x1, waiting for transfers between devices: 2.31 us -> 0.01 us  [exchange_and_step(): far_in = lax.ppermute(far, axes, far_route)]
    ppermute x1, starting transfers between devices: 4.55 us -> 2.47 us  [exchange_and_step(): near_in = lax.ppermute(near, axes, near_route)]
    pallas_call x6, Pallas kernels: 5.57 us -> 3.5 us  [call(): pl.pallas_call(kernel, name=name, out_shape=outs, in_specs=[SMEM] * smem...]
    pallas_call x0 -> x1, Pallas kernels: none -> 1.87 us  [shards(): pl.pallas_call(edges_kernel, name='edges', out_shape=[struct(FIELDS, laye...]
    ppermute x4, starting transfers between devices: 3.35 us -> 5.18 us  [the longest x2 2.56 us: exchange_and_step(): lax.ppermute(part, axes, (first_route, second_route)[i])]
  transfers between devices with their start and end apart: 7 -> 7, of which waited for: 4 -> 2; matrix products, arithmetic and copies ran while one was open for 0% -> 0% of each run, Pallas kernels for 14% -> 14%
where the time goes in v2:
time: 22.6 us; the launch traced here: 22.4 us
  starting transfers between devices  12.6 us (56%)
  Pallas kernels  5.36 us (24%)
  waiting for transfers between devices  2.79 us (12%)
  local copies, waits for them, and re-layouts  0.7 us (3%)
  between operations  0.67 us (3%)
  loops' own time  0.29 us (1%)
    pallas_call x6, Pallas kernels, call(): pl.pallas_call(kernel, name=name, out_shape=outs, in_specs=[SMEM] * smem...  3.5 us
    ppermute x1, starting transfers between devices, exchange_and_step(): far_in = lax.ppermute(far, axes, far_route)  3.09 us
    ppermute x2, starting transfers between devices, exchange_and_step(): lax.ppermute(part, axes, (first_route, second_route)[i])  2.56 us
    ppermute x1, starting transfers between devices, exchange_and_step(): second = lax.ppermute(for_second, axes, second_route)  2.55 us
    ppermute x1, starting transfers between devices, exchange_and_step(): near_in = lax.ppermute(near, axes, near_route)  2.47 us
    ppermute x1, waiting for transfers between devices, exchange_and_step(): second = lax.ppermute(for_second, axes, second_route)  2.19 us
    pallas_call x1, Pallas kernels, shards(): pl.pallas_call(edges_kernel, name='edges', out_shape=[struct(FIELDS, laye...  1.87 us
    ppermute x1, starting transfers between devices, exchange_and_step(): packed = lax.ppermute(packed, axes, turn_route)  1.86 us
  transfers between devices with their start and end apart: 7, of which 2 were waited for; matrix products, arithmetic and copies ran while one was open for 0% of the time, Pallas kernels for 14%

profile of v2, /device:TPU:0, one launch (start us, length us, event | category | flops | bytes accessed | tf_op | source)
XLA Modules:
  0.0 22.4 jit_solution(11492876613368980761)
XLA Ops:
  0.0 1.9 %edges.1 = (f32[8,4,16,128]{3,2,1,0:T(8,128)S(1)}, f32[3,16,128]{2,1,0:T(8,128)S(1)}, f32[4,16,128]{2,1,0:T(8,128)S(1)}, f32[4,16,128]{2,1,0:T(8,128)S(1)}, s32[...) custom-call(f32[4,16,128]{2,1,0:T(8,128)} %density.1, ...), custom_call_target="tpu_custom_call" | custom-call | tf_op jit(solution)/shard_map/edges/pallas_call | solution.py:569
  2.5 19.2 %conditional.1 = (f32[8,4,16,128]{3,2,1,0:T(8,128)S(1)}) conditional(s32[]{:T(128)} %bitcast, (f32[3,16,128]{2,1,0:T(8,128)S(1)}, f32[4,16,128]{2,1,0:T(8,128)S(1)}, f32[4,16,128]{2,1,0:T(8,128)S(1)}, f32[192,128]{1,0:T(8,128)S(1)}, f32[192,128]{1,0:T(8,128)S(1)}, /*index=5*/f32[8,4,16,128]{3,2,1,0:T(8,128)S(1)}, ...), branch_computations={%region_0.0_spmd, %region_1.0_spmd, %region_2.0_spmd, %region_3.0_... | conditional | bytes 3178784 | solution.py:589
  2.5 3.1 %collective-permute-start.1 = (f32[4,16,128]{2,1,0:T(8,128)S(1)}, f32[4,16,128]{2,1,0:T(8,128)S(1)}, u32[]{:S(2)}, u32[]{:S(2)}) collective-permute-start(f32[4,16,128]{2,1,0:T(8,128)S(1)} %get-tuple-element.70), channel_id=1, source_target_pairs={{0,1},{1,0},{2,3},{3,2},{4,5},{5,4},{6,7},{7,6},{8,9},{9,8},{10,11... | collective-permute-start | bytes 98312 | tf_op jit(solution)/shard_map/cond/branch_0_fun/ppermute | solution.py:507
  5.6 2.5 %collective-permute-start = (f32[3,16,128]{2,1,0:T(8,128)S(1)}, f32[3,16,128]{2,1,0:T(8,128)S(1)}, u32[]{:S(2)}, u32[]{:S(2)}) collective-permute-start(f32[3,16,128]{2,1,0:T(8,128)S(1)} %get-tuple-element.69), channel_id=1, source_target_pairs={{0,3},{1,2},{2,1},{3,0},{4,7},{5,6},{6,5},{7,4},{8,11},{9,10},{10,... | collective-permute-start | bytes 73736 | tf_op jit(solution)/shard_map/cond/branch_0_fun/ppermute | solution.py:508
  8.1 0.0 collective-permute-start.4
  8.1 2.6 %collective-permute-start.5 = (f32[192,128]{1,0:T(8,128)S(1)}, f32[192,128]{1,0:T(8,128)S(1)}, u32[]{:S(2)}, u32[]{:S(2)}) collective-permute-start(f32[192,128]{1,0:T(8,128)S(1)} %get-tuple-element.76), channel_id=1, source_target_pairs={{0,28},{1,29},{2,30},{3,31},{4,8},{5,9},{6,10},{7,11},{8,4},{9,5},... | collective-permute-start | bytes 294920 | tf_op jit(solution)/shard_map/cond/branch_0_fun/ppermute | solution.py:509
  10.7 0.6 %collective-permute-done.near = f32[3,16,128]{2,1,0:T(8,128)S(1)} collective-permute-done((f32[3,16,128]{2,1,0:T(8,128)S(1)}, f32[3,16,128]{2,1,0:T(8,128)S(1)}, u32[]{:S(2)}, u32[]{:S(2)}) %collective-permute-start) | collective-permute-done | bytes 24608 | tf_op jit(solution)/shard_map/cond/branch_0_fun/ppermute | solution.py:508
  11.3 0.0 collective-permute-done.1.far
  11.3 0.1 join.4
  11.4 0.1 collective-permute-start.2
  11.5 2.5 %collective-permute-start.3 = (f32[16,8,128]{2,1,0:T(8,128)S(1)}, f32[16,8,128]{2,1,0:T(8,128)S(1)}, u32[]{:S(2)}, u32[]{:S(2)}) collective-permute-start(f32[16,8,128]{2,1,0:T(8,128)S(1)} %get-tuple-element.73), channel_id=1, source_target_pairs={{0,28},{1,29},{2,30},{3,31},{4,8},{5,9},{6,10},{7,11},{8,4},{9,5},... | collective-permute-start | bytes 196616 | tf_op jit(solution)/shard_map/cond/branch_0_fun/ppermute | solution.py:520
  14.0 0.0 collective-permute-done.2.first
  14.0 2.2 %collective-permute-done.3.second = f32[16,8,128]{2,1,0:T(8,128)S(1)} collective-permute-done((f32[16,8,128]{2,1,0:T(8,128)S(1)}, f32[16,8,128]{2,1,0:T(8,128)S(1)}, u32[]{:S(2)}, u32[]{:S(2)}) %collective-permute-start.3) | collective-permute-done | bytes 65568 | tf_op jit(solution)/shard_map/cond/branch_0_fun/ppermute | solution.py:520
  16.2 0.5 %far.4 = f32[2,16,128]{2,1,0:T(8,128)S(1)} custom-call(s32[8,128]{1,0:T(8,128)S(1)} %get-tuple-element.66.shifts.offsets, f32[4,16,128]{2,1,0:T(8,128)S(1)} %get-tuple-element.71.own, f32[16,8,128]{2,1,0:T(8,128)S(1)} %collective-permute-done.2.first, f32[16,8,128]{2,1,0:T(8,128)S(1)} %collective-permute-done.3.second), custom_call_target="tpu_custom_call" | custom-call | bytes 262144 | tf_op jit(solution)/shard_map/cond/branch_0_fun/far/pallas_call | solution.py:457
  16.7 1.9 %collective-permute-start.6 = (f32[2,16,128]{2,1,0:T(8,128)S(1)}, f32[2,16,128]{2,1,0:T(8,128)S(1)}, u32[]{:S(2)}, u32[]{:S(2)}) collective-permute-start(f32[2,16,128]{2,1,0:T(8,128)S(1)} %far.4), channel_id=1, source_target_pairs={{0,16},{1,17},{2,18},{3,19},{4,20},{5,21},{6,22},{7,23},{8,24},{9,... | collective-permute-start | bytes 49160 | tf_op jit(solution)/shard_map/cond/branch_0_fun/ppermute | solution.py:542
  18.6 0.0 collective-permute-done.4.first
  18.6 0.0 collective-permute-done.5.second
  18.6 1.0 %first_section.4.partial = f32[8,4,32,128]{3,2,1,0:T(8,128)S(1)} custom-call(f32[8,4,16,128]{3,2,1,0:T(8,128)S(1)} %get-tuple-element.64.state, f32[192,128]{1,0:T(8,128)S(1)} %collective-permute-done.4.first, f32[192,128]{1,0:T(8,128)S(1)} %collective-permute-done.5.second), custom_call_target="tpu_custom_call" | custom-call | bytes 262144 | tf_op jit(solution)/shard_map/cond/branch_0_fun/first_section/pallas_call | solution.py:457
  19.6 1.0 %first_ends.4 = (f32[8,4,32,128]{3,2,1,0:T(8,128)S(1)}, f32[8,16,128]{2,1,0:T(8,128)S(1)}) custom-call(s32[8,128]{1,0:T(8,128)S(1)} %get-tuple-element.66.shifts.offsets, f32[8,4,16,128]{3,2,1,0:T(8,128)S(1)} %get-tuple-element.64.state, f32[4,16,128]{2,1,0:T(8,128)S(1)} %get-tuple-element.71.own, f32[16,8,128]{2,1,0:T(8,128)S(1)} %collective-permute-done.2.first, ...), custom_call_target="tpu_custom_call" | custom-call | bytes 262144 | tf_op jit(solution)/shard_map/cond/branch_0_fun/first_ends/pallas_call | solution.py:457
  20.6 0.6 %second_section.4.partial = f32[8,4,16,128]{3,2,1,0:T(8,128)S(1)} custom-call(f32[8,4,16,128]{3,2,1,0:T(8,128)S(1)} %get-tuple-element.64.state, f32[8,4,32,128]{3,2,1,0:T(8,128)S(1)} %get-tuple-element.77.section), custom_call_target="tpu_custom_call" | custom-call | bytes 262144 | tf_op jit(solution)/shard_map/cond/branch_0_fun/second_section/pallas_call | solution.py:457
  21.1 0.0 collective-permute-done.6.packed
  21.1 0.3 %second_ends.4 = f32[8,4,16,128]{3,2,1,0:T(8,128)S(1)} custom-call(f32[8,4,16,128]{3,2,1,0:T(8,128)S(1)} %second_section.4.partial, f32[8,16,128]{2,1,0:T(8,128)S(1)} %get-tuple-element.78.strips, f32[2,16,128]{2,1,0:T(8,128)S(1)} %collective-permute-done.6.packed), custom_call_target="tpu_custom_call" | custom-call | bytes 262144 | tf_op jit(solution)/shard_map/cond/branch_0_fun/second_ends/pallas_call | solution.py:457
  21.7 0.0 copy-start
  21.7 0.7 %copy-done = f32[8,4,16,128]{3,2,1,0:T(8,128)} copy-done((f32[8,4,16,128]{3,2,1,0:T(8,128)}, f32[8,4,16,128]{3,2,1,0:T(8,128)S(1)}, u32[]{:S(2)}) %copy-start) | copy-done | bytes 262168
Async XLA Ops:
  2.5 8.7 %collective-permute-start.1 = (f32[4,16,128]{2,1,0:T(8,128)S(1)}, f32[4,16,128]{2,1,0:T(8,128)S(1)}, u32[]{:S(2)}, u32[]{:S(2)}) collective-permute-start(f32[4,16,128]{2,1,0:T(8,128)S(1)} %get-tuple-element.70), channel_id=1, source_target_pairs={{0,1},{1,0},{2,3},{3,2},{4,5},{5,4},{6,7},{7,6},{8,9},{9,8},{10,11... | collective-permute-start | bytes 98312 | tf_op jit(solution)/shard_map/cond/branch_0_fun/ppermute | solution.py:507
  5.6 5.6 %collective-permute-start = (f32[3,16,128]{2,1,0:T(8,128)S(1)}, f32[3,16,128]{2,1,0:T(8,128)S(1)}, u32[]{:S(2)}, u32[]{:S(2)}) collective-permute-start(f32[3,16,128]{2,1,0:T(8,128)S(1)} %get-tuple-element.69), channel_id=1, source_target_pairs={{0,3},{1,2},{2,1},{3,0},{4,7},{5,6},{6,5},{7,4},{8,11},{9,10},{10,... | collective-permute-start | bytes 73736 | tf_op jit(solution)/shard_map/cond/branch_0_fun/ppermute | solution.py:508
  8.1 10.5 %collective-permute-start.4 = (f32[192,128]{1,0:T(8,128)S(1)}, f32[192,128]{1,0:T(8,128)S(1)}, u32[]{:S(2)}, u32[]{:S(2)}) collective-permute-start(f32[192,128]{1,0:T(8,128)S(1)} %get-tuple-element.75), channel_id=1, source_target_pairs={{0,4},{1,5},{2,6},{3,7},{4,0},{5,1},{6,2},{7,3},{8,12},{9,13},{10,... | collective-permute-start | bytes 294920 | tf_op jit(solution)/shard_map/cond/branch_0_fun/ppermute | solution.py:509
  8.1 10.5 %collective-permute-start.5 = (f32[192,128]{1,0:T(8,128)S(1)}, f32[192,128]{1,0:T(8,128)S(1)}, u32[]{:S(2)}, u32[]{:S(2)}) collective-permute-start(f32[192,128]{1,0:T(8,128)S(1)} %get-tuple-element.76), channel_id=1, source_target_pairs={{0,28},{1,29},{2,30},{3,31},{4,8},{5,9},{6,10},{7,11},{8,4},{9,5},... | collective-permute-start | bytes 294920 | tf_op jit(solution)/shard_map/cond/branch_0_fun/ppermute | solution.py:509
  11.4 2.6 %collective-permute-start.2 = (f32[16,8,128]{2,1,0:T(8,128)S(1)}, f32[16,8,128]{2,1,0:T(8,128)S(1)}, u32[]{:S(2)}, u32[]{:S(2)}) collective-permute-start(f32[16,8,128]{2,1,0:T(8,128)S(1)} %get-tuple-element.72), channel_id=1, source_target_pairs={{0,4},{1,5},{2,6},{3,7},{4,0},{5,1},{6,2},{7,3},{8,12},{9,13},{10,... | collective-permute-start | bytes 196616 | tf_op jit(solution)/shard_map/cond/branch_0_fun/ppermute | solution.py:519
  11.5 4.7 %collective-permute-start.3 = (f32[16,8,128]{2,1,0:T(8,128)S(1)}, f32[16,8,128]{2,1,0:T(8,128)S(1)}, u32[]{:S(2)}, u32[]{:S(2)}) collective-permute-start(f32[16,8,128]{2,1,0:T(8,128)S(1)} %get-tuple-element.73), channel_id=1, source_target_pairs={{0,28},{1,29},{2,30},{3,31},{4,8},{5,9},{6,10},{7,11},{8,4},{9,5},... | collective-permute-start | bytes 196616 | tf_op jit(solution)/shard_map/cond/branch_0_fun/ppermute | solution.py:520
  16.7 4.4 %collective-permute-start.6 = (f32[2,16,128]{2,1,0:T(8,128)S(1)}, f32[2,16,128]{2,1,0:T(8,128)S(1)}, u32[]{:S(2)}, u32[]{:S(2)}) collective-permute-start(f32[2,16,128]{2,1,0:T(8,128)S(1)} %far.4), channel_id=1, source_target_pairs={{0,16},{1,17},{2,18},{3,19},{4,20},{5,21},{6,22},{7,23},{8,24},{9,... | collective-permute-start | bytes 49160 | tf_op jit(solution)/shard_map/cond/branch_0_fun/ppermute | solution.py:542
  21.7 0.7 %copy-start = (f32[8,4,16,128]{3,2,1,0:T(8,128)}, f32[8,4,16,128]{3,2,1,0:T(8,128)S(1)}, u32[]{:S(2)}) copy-start(f32[8,4,16,128]{3,2,1,0:T(8,128)S(1)} %get-tuple-element.179) | copy-start | bytes 786436

commit v3 on v2

--- a/solution.py
+++ b/solution.py
@@ -153,7 +153,7 @@
 
 
 def edges_kernel(density, momentum, magnetic, tracer, offsets, state, near, far, pairs, index, shifts, *rest):
-    *bulks, held, sems = rest
+    *bulks, held, chosen, sems = rest
     layers, rows, cols = density.shape
     slot = cols // layers
     parts = (
@@ -166,6 +166,13 @@
     copies = [pltpu.make_async_copy(source, target, sems.at[i]) for i, (source, target) in enumerate(parts)]
     for copy in copies:
         copy.start()
+    copies[4].wait()
+    half = rows * lax.axis_size("az") // 2
+    chosen[0] = jnp.where(held[0] > rows - 4, 2, 0) + jnp.where(held[1] > rows - 4 + half, 1, 0)
+    chosen_copy = pltpu.make_async_copy(chosen, index, sems.at[5])
+    chosen_copy.start()
+    for i in range(2):
+        shifts[i : i + 1, :] = jnp.full((1, cols), held[i])
     odd, _, last = axis_place("rad")
     lane = lanes_of((rows, cols))
     width = 2 * REACH
@@ -201,11 +208,7 @@
             place = slice((f * layers + z) * width, (f * layers + z + 1) * width)
             bulks[0][place, :] = jnp.where(odd_az == 1, head, tail)
             bulks[1][place, :] = jnp.where(odd_az == 1, tail, head)
-    copies[4].wait()
-    half = rows * lax.axis_size("az") // 2
-    for i in range(2):
-        shifts[i : i + 1, :] = jnp.full((1, cols), held[i])
-    index[...] = jnp.full((1,), jnp.where(held[0] > rows - 4, 2, 0) + jnp.where(held[1] > rows - 4 + half, 1, 0))
+    chosen_copy.wait()
 
 
 def join_kernel(pairs, near, far, own, halo, first, second):
@@ -238,7 +241,7 @@
             out[tiles * parts + f] = halo[f, pl.ds(start, SUB), :]
 
 
-def far_kernel(offsets, own, first, second, packed, window, flows_ref, cells_ref, *, turn, wrap):
+def far_kernel(offsets, own, first, second, _, packed, window, flows_ref, cells_ref, *, turn, wrap):
     odd_az, _, _ = axis_place("az")
     _, _, last = axis_place("rad")
     tiles, rows, cols = own.shape
@@ -537,6 +540,7 @@
         own,
         first,
         second,
+        partial,
         scratch=[window] + [(FIELDS, rows + 3 * SUB, cols)] * 2,
     )
     packed = lax.ppermute(packed, axes, turn_route)
@@ -571,16 +575,16 @@
         name="edges",
         out_shape=[
             struct(FIELDS, layers, rows, cols),
-            struct(3, rows, cols),
             struct(4, rows, cols),
+            struct(6, rows, cols),
             struct(4, rows, cols),
             jax.ShapeDtypeStruct((1,), jnp.int32),
             jax.ShapeDtypeStruct((SUB, cols), jnp.int32),
         ]
         + [struct(FIELDS * layers * 2 * REACH, cols)] * 2,
         in_specs=[HBM] * 5,
-        out_specs=[VMEM] * 8,
-        scratch_shapes=[pltpu.SMEM((2,), jnp.int32), pltpu.SemaphoreType.DMA((5,))],
+        out_specs=[VMEM] * 4 + [HBM] + [VMEM] * 3,
+        scratch_shapes=[pltpu.SMEM((2,), jnp.int32), pltpu.SMEM((1,), jnp.int32), pltpu.SemaphoreType.DMA((6,))],
         compiler_params=pltpu.CompilerParams(vmem_limit_bytes=BIG),
     )(density, momentum, magnetic, tracer, offsets)
     branches = [

time: 22.6 us -> 21.6 us (0.956)
  waiting for transfers between devices: 2.79 us -> 2.28 us
  Pallas kernels: 5.36 us -> 4.86 us
    ppermute x1, waiting for transfers between devices: 2.19 us -> 1.16 us  [exchange_and_step(): second = lax.ppermute(for_second, axes, second_route)]
    pallas_call x1, Pallas kernels: 1.87 us -> 1.37 us  [shards(): pl.pallas_call(edges_kernel, name='edges', out_shape=[struct(FIELDS, laye...]
    ppermute x1, waiting for transfers between devices: 0.01 us -> 0.43 us  [exchange_and_step(): packed = lax.ppermute(packed, axes, turn_route)]
  transfers between devices with their start and end apart: 7 -> 7, of which waited for: 2 -> 3; matrix products, arithmetic and copies ran while one was open for 0% -> 0% of each run, Pallas kernels for 14% -> 12%
where the time goes in v3:
time: 21.6 us; the launch traced here: 21.4 us
  starting transfers between devices  12.6 us (58%)
  Pallas kernels  4.86 us (22%)
  waiting for transfers between devices  2.28 us (11%)
  local copies, waits for them, and re-layouts  0.7 us (3%)
  between operations  0.67 us (3%)
  loops' own time  0.29 us (1%)
    pallas_call x6, Pallas kernels, call(): pl.pallas_call(kernel, name=name, out_shape=outs, in_specs=[SMEM] * smem...  3.49 us
    ppermute x1, starting transfers between devices, exchange_and_step(): far_in = lax.ppermute(far, axes, far_route)  3.09 us
    ppermute x2, starting transfers between devices, exchange_and_step(): lax.ppermute(part, axes, (first_route, second_route)[i])  2.56 us
    ppermute x1, starting transfers between devices, exchange_and_step(): second = lax.ppermute(for_second, axes, second_route)  2.55 us
    ppermute x1, starting transfers between devices, exchange_and_step(): near_in = lax.ppermute(near, axes, near_route)  2.47 us
    ppermute x1, starting transfers between devices, exchange_and_step(): packed = lax.ppermute(packed, axes, turn_route)  1.86 us
    pallas_call x1, Pallas kernels, shards(): pl.pallas_call(edges_kernel, name='edges', out_shape=[struct(FIELDS, laye...  1.37 us
    ppermute x1, waiting for transfers between devices, exchange_and_step(): second = lax.ppermute(for_second, axes, second_route)  1.16 us
  transfers between devices with their start and end apart: 7, of which 3 were waited for; matrix products, arithmetic and copies ran while one was open for 0% of the time, Pallas kernels for 12%

profile of v3, /device:TPU:0, one launch (start us, length us, event | category | flops | bytes accessed | tf_op | source)
XLA Modules:
  0.0 21.4 jit_solution(17028911023979429917)
XLA Ops:
  0.0 1.4 %edges.1 = (f32[8,4,16,128]{3,2,1,0:T(8,128)S(1)}, f32[4,16,128]{2,1,0:T(8,128)S(1)}, f32[6,16,128]{2,1,0:T(8,128)S(1)}, f32[4,16,128]{2,1,0:T(8,128)S(1)}, s32[...) custom-call(f32[4,16,128]{2,1,0:T(8,128)} %density.1, ...), custom_call_target="tpu_custom_call" | custom-call | tf_op jit(solution)/shard_map/edges/pallas_call | solution.py:573
  2.0 18.7 %conditional.1 = (f32[8,4,16,128]{3,2,1,0:T(8,128)S(1)}) conditional(s32[]{:T(128)} %bitcast, (f32[4,16,128]{2,1,0:T(8,128)S(1)}, f32[6,16,128]{2,1,0:T(8,128)S(1)}, f32[4,16,128]{2,1,0:T(8,128)S(1)}, f32[192,128]{1,0:T(8,128)S(1)}, f32[192,128]{1,0:T(8,128)S(1)}, /*index=5*/f32[8,4,16,128]{3,2,1,0:T(8,128)S(1)}, ...), branch_computations={%region_0.0_spmd, %region_1.0_spmd, %region_2.0_spmd, %region_3.0_... | conditional | bytes 3277088 | solution.py:593
  2.0 3.1 %collective-permute-start.1 = (f32[6,16,128]{2,1,0:T(8,128)S(1)}, f32[6,16,128]{2,1,0:T(8,128)S(1)}, u32[]{:S(2)}, u32[]{:S(2)}) collective-permute-start(f32[6,16,128]{2,1,0:T(8,128)S(1)} %get-tuple-element.70), channel_id=1, source_target_pairs={{0,1},{1,0},{2,3},{3,2},{4,5},{5,4},{6,7},{7,6},{8,9},{9,8},{10,11... | collective-permute-start | bytes 147464 | tf_op jit(solution)/shard_map/cond/branch_0_fun/ppermute | solution.py:510
  5.1 2.5 %collective-permute-start = (f32[4,16,128]{2,1,0:T(8,128)S(1)}, f32[4,16,128]{2,1,0:T(8,128)S(1)}, u32[]{:S(2)}, u32[]{:S(2)}) collective-permute-start(f32[4,16,128]{2,1,0:T(8,128)S(1)} %get-tuple-element.69), channel_id=1, source_target_pairs={{0,3},{1,2},{2,1},{3,0},{4,7},{5,6},{6,5},{7,4},{8,11},{9,10},{10,... | collective-permute-start | bytes 98312 | tf_op jit(solution)/shard_map/cond/branch_0_fun/ppermute | solution.py:511
  7.6 0.0 collective-permute-start.4
  7.6 2.6 %collective-permute-start.5 = (f32[192,128]{1,0:T(8,128)S(1)}, f32[192,128]{1,0:T(8,128)S(1)}, u32[]{:S(2)}, u32[]{:S(2)}) collective-permute-start(f32[192,128]{1,0:T(8,128)S(1)} %get-tuple-element.76), channel_id=1, source_target_pairs={{0,28},{1,29},{2,30},{3,31},{4,8},{5,9},{6,10},{7,11},{8,4},{9,5},... | collective-permute-start | bytes 294920 | tf_op jit(solution)/shard_map/cond/branch_0_fun/ppermute | solution.py:512
  10.2 0.7 %collective-permute-done.near = f32[4,16,128]{2,1,0:T(8,128)S(1)} collective-permute-done((f32[4,16,128]{2,1,0:T(8,128)S(1)}, f32[4,16,128]{2,1,0:T(8,128)S(1)}, u32[]{:S(2)}, u32[]{:S(2)}) %collective-permute-start) | collective-permute-done | bytes 32800 | tf_op jit(solution)/shard_map/cond/branch_0_fun/ppermute | solution.py:511
  10.8 0.0 collective-permute-done.1.far
  10.8 0.1 join.4
  11.0 0.1 collective-permute-start.2
  11.1 2.5 %collective-permute-start.3 = (f32[16,8,128]{2,1,0:T(8,128)S(1)}, f32[16,8,128]{2,1,0:T(8,128)S(1)}, u32[]{:S(2)}, u32[]{:S(2)}) collective-permute-start(f32[16,8,128]{2,1,0:T(8,128)S(1)} %get-tuple-element.73), channel_id=1, source_target_pairs={{0,28},{1,29},{2,30},{3,31},{4,8},{5,9},{6,10},{7,11},{8,4},{9,5},... | collective-permute-start | bytes 196616 | tf_op jit(solution)/shard_map/cond/branch_0_fun/ppermute | solution.py:523
  13.6 0.0 collective-permute-done.4.first
  13.6 0.0 collective-permute-done.5.second
  13.6 1.0 %first_section.4.partial._ = f32[8,4,32,128]{3,2,1,0:T(8,128)S(1)} custom-call(f32[8,4,16,128]{3,2,1,0:T(8,128)S(1)} %get-tuple-element.64.state, f32[192,128]{1,0:T(8,128)S(1)} %collective-permute-done.4.first, f32[192,128]{1,0:T(8,128)S(1)} %collective-permute-done.5.second), custom_call_target="tpu_custom_call" | custom-call | bytes 262144 | tf_op jit(solution)/shard_map/cond/branch_0_fun/first_section/pallas_call | solution.py:460
  14.6 0.0 collective-permute-done.2.first
  14.6 1.2 %collective-permute-done.3.second = f32[16,8,128]{2,1,0:T(8,128)S(1)} collective-permute-done((f32[16,8,128]{2,1,0:T(8,128)S(1)}, f32[16,8,128]{2,1,0:T(8,128)S(1)}, u32[]{:S(2)}, u32[]{:S(2)}) %collective-permute-start.3) | collective-permute-done | bytes 65568 | tf_op jit(solution)/shard_map/cond/branch_0_fun/ppermute | solution.py:523
  15.8 0.5 %far.4 = f32[2,16,128]{2,1,0:T(8,128)S(1)} custom-call(s32[8,128]{1,0:T(8,128)S(1)} %get-tuple-element.66.shifts.offsets, f32[4,16,128]{2,1,0:T(8,128)S(1)} %get-tuple-element.71.own, f32[16,8,128]{2,1,0:T(8,128)S(1)} %collective-permute-done.2.first, f32[16,8,128]{2,1,0:T(8,128)S(1)} %collective-permute-done.3.second, ...), custom_call_target="tpu_custom_call" | custom-call | bytes 262144 | tf_op jit(solution)/shard_map/cond/branch_0_fun/far/pallas_call | solution.py:460
  16.3 1.9 %collective-permute-start.6 = (f32[2,16,128]{2,1,0:T(8,128)S(1)}, f32[2,16,128]{2,1,0:T(8,128)S(1)}, u32[]{:S(2)}, u32[]{:S(2)}) collective-permute-start(f32[2,16,128]{2,1,0:T(8,128)S(1)} %far.4), channel_id=1, source_target_pairs={{0,16},{1,17},{2,18},{3,19},{4,20},{5,21},{6,22},{7,23},{8,24},{9,... | collective-permute-start | bytes 49160 | tf_op jit(solution)/shard_map/cond/branch_0_fun/ppermute | solution.py:546
  18.2 1.0 %first_ends.4 = (f32[8,4,32,128]{3,2,1,0:T(8,128)S(1)}, f32[8,16,128]{2,1,0:T(8,128)S(1)}) custom-call(s32[8,128]{1,0:T(8,128)S(1)} %get-tuple-element.66.shifts.offsets, f32[8,4,16,128]{3,2,1,0:T(8,128)S(1)} %get-tuple-element.64.state, f32[4,16,128]{2,1,0:T(8,128)S(1)} %get-tuple-element.71.own, f32[16,8,128]{2,1,0:T(8,128)S(1)} %collective-permute-done.2.first, ...), custom_call_target="tpu_custom_call" | custom-call | bytes 262144 | tf_op jit(solution)/shard_map/cond/branch_0_fun/first_ends/pallas_call | solution.py:460
  19.1 0.6 %second_section.4.partial = f32[8,4,16,128]{3,2,1,0:T(8,128)S(1)} custom-call(f32[8,4,16,128]{3,2,1,0:T(8,128)S(1)} %get-tuple-element.64.state, f32[8,4,32,128]{3,2,1,0:T(8,128)S(1)} %get-tuple-element.77.section), custom_call_target="tpu_custom_call" | custom-call | bytes 262144 | tf_op jit(solution)/shard_map/cond/branch_0_fun/second_section/pallas_call | solution.py:460
  19.7 0.4 %collective-permute-done.6.packed = f32[2,16,128]{2,1,0:T(8,128)S(1)} collective-permute-done((f32[2,16,128]{2,1,0:T(8,128)S(1)}, f32[2,16,128]{2,1,0:T(8,128)S(1)}, u32[]{:S(2)}, u32[]{:S(2)}) %collective-permute-start.6) | collective-permute-done | bytes 16416 | tf_op jit(solution)/shard_map/cond/branch_0_fun/ppermute | solution.py:546
  20.1 0.3 %second_ends.4 = f32[8,4,16,128]{3,2,1,0:T(8,128)S(1)} custom-call(f32[8,4,16,128]{3,2,1,0:T(8,128)S(1)} %second_section.4.partial, f32[8,16,128]{2,1,0:T(8,128)S(1)} %get-tuple-element.78.strips, f32[2,16,128]{2,1,0:T(8,128)S(1)} %collective-permute-done.6.packed), custom_call_target="tpu_custom_call" | custom-call | bytes 262144 | tf_op jit(solution)/shard_map/cond/branch_0_fun/second_ends/pallas_call | solution.py:460
  20.7 0.0 copy-start
  20.7 0.7 %copy-done = f32[8,4,16,128]{3,2,1,0:T(8,128)} copy-done((f32[8,4,16,128]{3,2,1,0:T(8,128)}, f32[8,4,16,128]{3,2,1,0:T(8,128)S(1)}, u32[]{:S(2)}) %copy-start) | copy-done | bytes 262168
Async XLA Ops:
  2.0 8.8 %collective-permute-start.1 = (f32[6,16,128]{2,1,0:T(8,128)S(1)}, f32[6,16,128]{2,1,0:T(8,128)S(1)}, u32[]{:S(2)}, u32[]{:S(2)}) collective-permute-start(f32[6,16,128]{2,1,0:T(8,128)S(1)} %get-tuple-element.70), channel_id=1, source_target_pairs={{0,1},{1,0},{2,3},{3,2},{4,5},{5,4},{6,7},{7,6},{8,9},{9,8},{10,11... | collective-permute-start | bytes 147464 | tf_op jit(solution)/shard_map/cond/branch_0_fun/ppermute | solution.py:510
  5.1 5.7 %collective-permute-start = (f32[4,16,128]{2,1,0:T(8,128)S(1)}, f32[4,16,128]{2,1,0:T(8,128)S(1)}, u32[]{:S(2)}, u32[]{:S(2)}) collective-permute-start(f32[4,16,128]{2,1,0:T(8,128)S(1)} %get-tuple-element.69), channel_id=1, source_target_pairs={{0,3},{1,2},{2,1},{3,0},{4,7},{5,6},{6,5},{7,4},{8,11},{9,10},{10,... | collective-permute-start | bytes 98312 | tf_op jit(solution)/shard_map/cond/branch_0_fun/ppermute | solution.py:511
  7.6 6.0 %collective-permute-start.4 = (f32[192,128]{1,0:T(8,128)S(1)}, f32[192,128]{1,0:T(8,128)S(1)}, u32[]{:S(2)}, u32[]{:S(2)}) collective-permute-start(f32[192,128]{1,0:T(8,128)S(1)} %get-tuple-element.75), channel_id=1, source_target_pairs={{0,4},{1,5},{2,6},{3,7},{4,0},{5,1},{6,2},{7,3},{8,12},{9,13},{10,... | collective-permute-start | bytes 294920 | tf_op jit(solution)/shard_map/cond/branch_0_fun/ppermute | solution.py:512
  7.6 6.0 %collective-permute-start.5 = (f32[192,128]{1,0:T(8,128)S(1)}, f32[192,128]{1,0:T(8,128)S(1)}, u32[]{:S(2)}, u32[]{:S(2)}) collective-permute-start(f32[192,128]{1,0:T(8,128)S(1)} %get-tuple-element.76), channel_id=1, source_target_pairs={{0,28},{1,29},{2,30},{3,31},{4,8},{5,9},{6,10},{7,11},{8,4},{9,5},... | collective-permute-start | bytes 294920 | tf_op jit(solution)/shard_map/cond/branch_0_fun/ppermute | solution.py:512
  11.0 3.6 %collective-permute-start.2 = (f32[16,8,128]{2,1,0:T(8,128)S(1)}, f32[16,8,128]{2,1,0:T(8,128)S(1)}, u32[]{:S(2)}, u32[]{:S(2)}) collective-permute-start(f32[16,8,128]{2,1,0:T(8,128)S(1)} %get-tuple-element.72), channel_id=1, source_target_pairs={{0,4},{1,5},{2,6},{3,7},{4,0},{5,1},{6,2},{7,3},{8,12},{9,13},{10,... | collective-permute-start | bytes 196616 | tf_op jit(solution)/shard_map/cond/branch_0_fun/ppermute | solution.py:522
  11.1 4.7 %collective-permute-start.3 = (f32[16,8,128]{2,1,0:T(8,128)S(1)}, f32[16,8,128]{2,1,0:T(8,128)S(1)}, u32[]{:S(2)}, u32[]{:S(2)}) collective-permute-start(f32[16,8,128]{2,1,0:T(8,128)S(1)} %get-tuple-element.73), channel_id=1, source_target_pairs={{0,28},{1,29},{2,30},{3,31},{4,8},{5,9},{6,10},{7,11},{8,4},{9,5},... | collective-permute-start | bytes 196616 | tf_op jit(solution)/shard_map/cond/branch_0_fun/ppermute | solution.py:523
  16.3 3.8 %collective-permute-start.6 = (f32[2,16,128]{2,1,0:T(8,128)S(1)}, f32[2,16,128]{2,1,0:T(8,128)S(1)}, u32[]{:S(2)}, u32[]{:S(2)}) collective-permute-start(f32[2,16,128]{2,1,0:T(8,128)S(1)} %far.4), channel_id=1, source_target_pairs={{0,16},{1,17},{2,18},{3,19},{4,20},{5,21},{6,22},{7,23},{8,24},{9,... | collective-permute-start | bytes 49160 | tf_op jit(solution)/shard_map/cond/branch_0_fun/ppermute | solution.py:546
  20.7 0.7 %copy-start = (f32[8,4,16,128]{3,2,1,0:T(8,128)}, f32[8,4,16,128]{3,2,1,0:T(8,128)S(1)}, u32[]{:S(2)}) copy-start(f32[8,4,16,128]{3,2,1,0:T(8,128)S(1)} %get-tuple-element.179) | copy-start | bytes 786436

commit v4 on v3

--- a/solution.py
+++ b/solution.py
@@ -153,7 +153,7 @@
 
 
 def edges_kernel(density, momentum, magnetic, tracer, offsets, state, near, far, pairs, index, shifts, *rest):
-    *bulks, held, chosen, sems = rest
+    *bulks, held, sems = rest
     layers, rows, cols = density.shape
     slot = cols // layers
     parts = (
@@ -168,9 +168,7 @@
         copy.start()
     copies[4].wait()
     half = rows * lax.axis_size("az") // 2
-    chosen[0] = jnp.where(held[0] > rows - 4, 2, 0) + jnp.where(held[1] > rows - 4 + half, 1, 0)
-    chosen_copy = pltpu.make_async_copy(chosen, index, sems.at[5])
-    chosen_copy.start()
+    index[0] = jnp.where(held[0] > rows - 4, 2, 0) + jnp.where(held[1] > rows - 4 + half, 1, 0)
     for i in range(2):
         shifts[i : i + 1, :] = jnp.full((1, cols), held[i])
     odd, _, last = axis_place("rad")
@@ -208,7 +206,6 @@
             place = slice((f * layers + z) * width, (f * layers + z + 1) * width)
             bulks[0][place, :] = jnp.where(odd_az == 1, head, tail)
             bulks[1][place, :] = jnp.where(odd_az == 1, tail, head)
-    chosen_copy.wait()
 
 
 def join_kernel(pairs, near, far, own, halo, first, second):
@@ -578,13 +575,13 @@
             struct(4, rows, cols),
             struct(6, rows, cols),
             struct(4, rows, cols),
-            jax.ShapeDtypeStruct((1,), jnp.int32),
+            pltpu.SMEM((1,), jnp.int32),
             jax.ShapeDtypeStruct((SUB, cols), jnp.int32),
         ]
         + [struct(FIELDS * layers * 2 * REACH, cols)] * 2,
         in_specs=[HBM] * 5,
-        out_specs=[VMEM] * 4 + [HBM] + [VMEM] * 3,
-        scratch_shapes=[pltpu.SMEM((2,), jnp.int32), pltpu.SMEM((1,), jnp.int32), pltpu.SemaphoreType.DMA((6,))],
+        out_specs=[VMEM] * 4 + [SMEM] + [VMEM] * 3,
+        scratch_shapes=[pltpu.SMEM((2,), jnp.int32), pltpu.SemaphoreType.DMA((5,))],
         compiler_params=pltpu.CompilerParams(vmem_limit_bytes=BIG),
     )(density, momentum, magnetic, tracer, offsets)
     branches = [

time: 21.6 us -> 20.9 us (0.968)
  between operations: 0.67 us -> 0.03 us
  transfers between devices with their start and end apart: 7 -> 7, of which waited for: 3 -> 3; matrix products, arithmetic and copies ran while one was open for 0% -> 0% of each run, Pallas kernels for 12% -> 13%
where the time goes in v4:
time: 20.9 us; the launch traced here: 20.7 us
  starting transfers between devices  12.6 us (60%)
  Pallas kernels  4.83 us (23%)
  waiting for transfers between devices  2.28 us (11%)
  local copies, waits for them, and re-layouts  0.7 us (3%)
  loops' own time  0.29 us (1%)
    pallas_call x6, Pallas kernels, call(): pl.pallas_call(kernel, name=name, out_shape=outs, in_specs=[SMEM] * smem...  3.49 us
    ppermute x1, starting transfers between devices, exchange_and_step(): far_in = lax.ppermute(far, axes, far_route)  3.09 us
    ppermute x2, starting transfers between devices, exchange_and_step(): lax.ppermute(part, axes, (first_route, second_route)[i])  2.56 us
    ppermute x1, starting transfers between devices, exchange_and_step(): second = lax.ppermute(for_second, axes, second_route)  2.55 us
    ppermute x1, starting transfers between devices, exchange_and_step(): near_in = lax.ppermute(near, axes, near_route)  2.47 us
    ppermute x1, starting transfers between devices, exchange_and_step(): packed = lax.ppermute(packed, axes, turn_route)  1.86 us
    pallas_call x1, Pallas kernels, shards(): pl.pallas_call(edges_kernel, name='edges', out_shape=[struct(FIELDS, laye...  1.34 us
    ppermute x1, waiting for transfers between devices, exchange_and_step(): second = lax.ppermute(for_second, axes, second_route)  1.16 us
  transfers between devices with their start and end apart: 7, of which 3 were waited for; matrix products, arithmetic and copies ran while one was open for 0% of the time, Pallas kernels for 13%

profile of v4, /device:TPU:0, one launch (start us, length us, event | category | flops | bytes accessed | tf_op | source)
XLA Modules:
  0.0 20.7 jit_solution(5886853776036527552)
XLA Ops:
  0.0 1.3 %edges.1 = (f32[8,4,16,128]{3,2,1,0:T(8,128)S(1)}, f32[4,16,128]{2,1,0:T(8,128)S(1)}, f32[6,16,128]{2,1,0:T(8,128)S(1)}, f32[4,16,128]{2,1,0:T(8,128)S(1)}, s32[...) custom-call(f32[4,16,128]{2,1,0:T(8,128)} %density.1, ...), custom_call_target="tpu_custom_call" | custom-call | tf_op jit(solution)/shard_map/edges/pallas_call | solution.py:570
  1.4 18.7 %conditional.1 = (f32[8,4,16,128]{3,2,1,0:T(8,128)S(1)}) conditional(s32[]{:T(128)} %bitcast, (f32[4,16,128]{2,1,0:T(8,128)S(1)}, f32[6,16,128]{2,1,0:T(8,128)S(1)}, f32[4,16,128]{2,1,0:T(8,128)S(1)}, f32[192,128]{1,0:T(8,128)S(1)}, f32[192,128]{1,0:T(8,128)S(1)}, /*index=5*/f32[8,4,16,128]{3,2,1,0:T(8,128)S(1)}, ...), branch_computations={%region_0.0_spmd, %region_1.0_spmd, %region_2.0_spmd, %region_3.0_... | conditional | bytes 3277088 | solution.py:590
  1.4 3.1 %collective-permute-start.1 = (f32[6,16,128]{2,1,0:T(8,128)S(1)}, f32[6,16,128]{2,1,0:T(8,128)S(1)}, u32[]{:S(2)}, u32[]{:S(2)}) collective-permute-start(f32[6,16,128]{2,1,0:T(8,128)S(1)} %get-tuple-element.70), channel_id=1, source_target_pairs={{0,1},{1,0},{2,3},{3,2},{4,5},{5,4},{6,7},{7,6},{8,9},{9,8},{10,11... | collective-permute-start | bytes 147464 | tf_op jit(solution)/shard_map/cond/branch_0_fun/ppermute | solution.py:507
  4.5 2.5 %collective-permute-start = (f32[4,16,128]{2,1,0:T(8,128)S(1)}, f32[4,16,128]{2,1,0:T(8,128)S(1)}, u32[]{:S(2)}, u32[]{:S(2)}) collective-permute-start(f32[4,16,128]{2,1,0:T(8,128)S(1)} %get-tuple-element.69), channel_id=1, source_target_pairs={{0,3},{1,2},{2,1},{3,0},{4,7},{5,6},{6,5},{7,4},{8,11},{9,10},{10,... | collective-permute-start | bytes 98312 | tf_op jit(solution)/shard_map/cond/branch_0_fun/ppermute | solution.py:508
  6.9 0.0 collective-permute-start.4
  6.9 2.6 %collective-permute-start.5 = (f32[192,128]{1,0:T(8,128)S(1)}, f32[192,128]{1,0:T(8,128)S(1)}, u32[]{:S(2)}, u32[]{:S(2)}) collective-permute-start(f32[192,128]{1,0:T(8,128)S(1)} %get-tuple-element.76), channel_id=1, source_target_pairs={{0,28},{1,29},{2,30},{3,31},{4,8},{5,9},{6,10},{7,11},{8,4},{9,5},... | collective-permute-start | bytes 294920 | tf_op jit(solution)/shard_map/cond/branch_0_fun/ppermute | solution.py:509
  9.5 0.7 %collective-permute-done.near = f32[4,16,128]{2,1,0:T(8,128)S(1)} collective-permute-done((f32[4,16,128]{2,1,0:T(8,128)S(1)}, f32[4,16,128]{2,1,0:T(8,128)S(1)}, u32[]{:S(2)}, u32[]{:S(2)}) %collective-permute-start) | collective-permute-done | bytes 32800 | tf_op jit(solution)/shard_map/cond/branch_0_fun/ppermute | solution.py:508
  10.2 0.0 collective-permute-done.1.far
  10.2 0.1 join.4
  10.3 0.1 collective-permute-start.2
  10.4 2.5 %collective-permute-start.3 = (f32[16,8,128]{2,1,0:T(8,128)S(1)}, f32[16,8,128]{2,1,0:T(8,128)S(1)}, u32[]{:S(2)}, u32[]{:S(2)}) collective-permute-start(f32[16,8,128]{2,1,0:T(8,128)S(1)} %get-tuple-element.73), channel_id=1, source_target_pairs={{0,28},{1,29},{2,30},{3,31},{4,8},{5,9},{6,10},{7,11},{8,4},{9,5},... | collective-permute-start | bytes 196616 | tf_op jit(solution)/shard_map/cond/branch_0_fun/ppermute | solution.py:520
  12.9 0.0 collective-permute-done.4.first
  12.9 0.0 collective-permute-done.5.second
  12.9 1.0 %first_section.4.partial._ = f32[8,4,32,128]{3,2,1,0:T(8,128)S(1)} custom-call(f32[8,4,16,128]{3,2,1,0:T(8,128)S(1)} %get-tuple-element.64.state, f32[192,128]{1,0:T(8,128)S(1)} %collective-permute-done.4.first, f32[192,128]{1,0:T(8,128)S(1)} %collective-permute-done.5.second), custom_call_target="tpu_custom_call" | custom-call | bytes 262144 | tf_op jit(solution)/shard_map/cond/branch_0_fun/first_section/pallas_call | solution.py:457
  14.0 0.0 collective-permute-done.2.first
  14.0 1.2 %collective-permute-done.3.second = f32[16,8,128]{2,1,0:T(8,128)S(1)} collective-permute-done((f32[16,8,128]{2,1,0:T(8,128)S(1)}, f32[16,8,128]{2,1,0:T(8,128)S(1)}, u32[]{:S(2)}, u32[]{:S(2)}) %collective-permute-start.3) | collective-permute-done | bytes 65568 | tf_op jit(solution)/shard_map/cond/branch_0_fun/ppermute | solution.py:520
  15.1 0.5 %far.4 = f32[2,16,128]{2,1,0:T(8,128)S(1)} custom-call(s32[8,128]{1,0:T(8,128)S(1)} %get-tuple-element.66.shifts.offsets, f32[4,16,128]{2,1,0:T(8,128)S(1)} %get-tuple-element.71.own, f32[16,8,128]{2,1,0:T(8,128)S(1)} %collective-permute-done.2.first, f32[16,8,128]{2,1,0:T(8,128)S(1)} %collective-permute-done.3.second, ...), custom_call_target="tpu_custom_call" | custom-call | bytes 262144 | tf_op jit(solution)/shard_map/cond/branch_0_fun/far/pallas_call | solution.py:457
  15.6 1.9 %collective-permute-start.6 = (f32[2,16,128]{2,1,0:T(8,128)S(1)}, f32[2,16,128]{2,1,0:T(8,128)S(1)}, u32[]{:S(2)}, u32[]{:S(2)}) collective-permute-start(f32[2,16,128]{2,1,0:T(8,128)S(1)} %far.4), channel_id=1, source_target_pairs={{0,16},{1,17},{2,18},{3,19},{4,20},{5,21},{6,22},{7,23},{8,24},{9,... | collective-permute-start | bytes 49160 | tf_op jit(solution)/shard_map/cond/branch_0_fun/ppermute | solution.py:543
  17.5 1.0 %first_ends.4 = (f32[8,4,32,128]{3,2,1,0:T(8,128)S(1)}, f32[8,16,128]{2,1,0:T(8,128)S(1)}) custom-call(s32[8,128]{1,0:T(8,128)S(1)} %get-tuple-element.66.shifts.offsets, f32[8,4,16,128]{3,2,1,0:T(8,128)S(1)} %get-tuple-element.64.state, f32[4,16,128]{2,1,0:T(8,128)S(1)} %get-tuple-element.71.own, f32[16,8,128]{2,1,0:T(8,128)S(1)} %collective-permute-done.2.first, ...), custom_call_target="tpu_custom_call" | custom-call | bytes 262144 | tf_op jit(solution)/shard_map/cond/branch_0_fun/first_ends/pallas_call | solution.py:457
  18.5 0.6 %second_section.4.partial = f32[8,4,16,128]{3,2,1,0:T(8,128)S(1)} custom-call(f32[8,4,16,128]{3,2,1,0:T(8,128)S(1)} %get-tuple-element.64.state, f32[8,4,32,128]{3,2,1,0:T(8,128)S(1)} %get-tuple-element.77.section), custom_call_target="tpu_custom_call" | custom-call | bytes 262144 | tf_op jit(solution)/shard_map/cond/branch_0_fun/second_section/pallas_call | solution.py:457
  19.0 0.4 %collective-permute-done.6.packed = f32[2,16,128]{2,1,0:T(8,128)S(1)} collective-permute-done((f32[2,16,128]{2,1,0:T(8,128)S(1)}, f32[2,16,128]{2,1,0:T(8,128)S(1)}, u32[]{:S(2)}, u32[]{:S(2)}) %collective-permute-start.6) | collective-permute-done | bytes 16416 | tf_op jit(solution)/shard_map/cond/branch_0_fun/ppermute | solution.py:543
  19.5 0.3 %second_ends.4 = f32[8,4,16,128]{3,2,1,0:T(8,128)S(1)} custom-call(f32[8,4,16,128]{3,2,1,0:T(8,128)S(1)} %second_section.4.partial, f32[8,16,128]{2,1,0:T(8,128)S(1)} %get-tuple-element.78.strips, f32[2,16,128]{2,1,0:T(8,128)S(1)} %collective-permute-done.6.packed), custom_call_target="tpu_custom_call" | custom-call | bytes 262144 | tf_op jit(solution)/shard_map/cond/branch_0_fun/second_ends/pallas_call | solution.py:457
  20.0 0.0 copy-start
  20.0 0.7 %copy-done = f32[8,4,16,128]{3,2,1,0:T(8,128)} copy-done((f32[8,4,16,128]{3,2,1,0:T(8,128)}, f32[8,4,16,128]{3,2,1,0:T(8,128)S(1)}, u32[]{:S(2)}) %copy-start) | copy-done | bytes 262168
Async XLA Ops:
  1.4 8.8 %collective-permute-start.1 = (f32[6,16,128]{2,1,0:T(8,128)S(1)}, f32[6,16,128]{2,1,0:T(8,128)S(1)}, u32[]{:S(2)}, u32[]{:S(2)}) collective-permute-start(f32[6,16,128]{2,1,0:T(8,128)S(1)} %get-tuple-element.70), channel_id=1, source_target_pairs={{0,1},{1,0},{2,3},{3,2},{4,5},{5,4},{6,7},{7,6},{8,9},{9,8},{10,11... | collective-permute-start | bytes 147464 | tf_op jit(solution)/shard_map/cond/branch_0_fun/ppermute | solution.py:507
  4.5 5.7 %collective-permute-start = (f32[4,16,128]{2,1,0:T(8,128)S(1)}, f32[4,16,128]{2,1,0:T(8,128)S(1)}, u32[]{:S(2)}, u32[]{:S(2)}) collective-permute-start(f32[4,16,128]{2,1,0:T(8,128)S(1)} %get-tuple-element.69), channel_id=1, source_target_pairs={{0,3},{1,2},{2,1},{3,0},{4,7},{5,6},{6,5},{7,4},{8,11},{9,10},{10,... | collective-permute-start | bytes 98312 | tf_op jit(solution)/shard_map/cond/branch_0_fun/ppermute | solution.py:508
  6.9 6.0 %collective-permute-start.4 = (f32[192,128]{1,0:T(8,128)S(1)}, f32[192,128]{1,0:T(8,128)S(1)}, u32[]{:S(2)}, u32[]{:S(2)}) collective-permute-start(f32[192,128]{1,0:T(8,128)S(1)} %get-tuple-element.75), channel_id=1, source_target_pairs={{0,4},{1,5},{2,6},{3,7},{4,0},{5,1},{6,2},{7,3},{8,12},{9,13},{10,... | collective-permute-start | bytes 294920 | tf_op jit(solution)/shard_map/cond/branch_0_fun/ppermute | solution.py:509
  6.9 6.0 %collective-permute-start.5 = (f32[192,128]{1,0:T(8,128)S(1)}, f32[192,128]{1,0:T(8,128)S(1)}, u32[]{:S(2)}, u32[]{:S(2)}) collective-permute-start(f32[192,128]{1,0:T(8,128)S(1)} %get-tuple-element.76), channel_id=1, source_target_pairs={{0,28},{1,29},{2,30},{3,31},{4,8},{5,9},{6,10},{7,11},{8,4},{9,5},... | collective-permute-start | bytes 294920 | tf_op jit(solution)/shard_map/cond/branch_0_fun/ppermute | solution.py:509
  10.3 3.6 %collective-permute-start.2 = (f32[16,8,128]{2,1,0:T(8,128)S(1)}, f32[16,8,128]{2,1,0:T(8,128)S(1)}, u32[]{:S(2)}, u32[]{:S(2)}) collective-permute-start(f32[16,8,128]{2,1,0:T(8,128)S(1)} %get-tuple-element.72), channel_id=1, source_target_pairs={{0,4},{1,5},{2,6},{3,7},{4,0},{5,1},{6,2},{7,3},{8,12},{9,13},{10,... | collective-permute-start | bytes 196616 | tf_op jit(solution)/shard_map/cond/branch_0_fun/ppermute | solution.py:519
  10.4 4.7 %collective-permute-start.3 = (f32[16,8,128]{2,1,0:T(8,128)S(1)}, f32[16,8,128]{2,1,0:T(8,128)S(1)}, u32[]{:S(2)}, u32[]{:S(2)}) collective-permute-start(f32[16,8,128]{2,1,0:T(8,128)S(1)} %get-tuple-element.73), channel_id=1, source_target_pairs={{0,28},{1,29},{2,30},{3,31},{4,8},{5,9},{6,10},{7,11},{8,4},{9,5},... | collective-permute-start | bytes 196616 | tf_op jit(solution)/shard_map/cond/branch_0_fun/ppermute | solution.py:520
  15.6 3.8 %collective-permute-start.6 = (f32[2,16,128]{2,1,0:T(8,128)S(1)}, f32[2,16,128]{2,1,0:T(8,128)S(1)}, u32[]{:S(2)}, u32[]{:S(2)}) collective-permute-start(f32[2,16,128]{2,1,0:T(8,128)S(1)} %far.4), channel_id=1, source_target_pairs={{0,16},{1,17},{2,18},{3,19},{4,20},{5,21},{6,22},{7,23},{8,24},{9,... | collective-permute-start | bytes 49160 | tf_op jit(solution)/shard_map/cond/branch_0_fun/ppermute | solution.py:543
  20.0 0.7 %copy-start = (f32[8,4,16,128]{3,2,1,0:T(8,128)}, f32[8,4,16,128]{3,2,1,0:T(8,128)S(1)}, u32[]{:S(2)}) copy-start(f32[8,4,16,128]{3,2,1,0:T(8,128)S(1)} %get-tuple-element.179) | copy-start | bytes 786436

commit v5 on v4

--- a/solution.py
+++ b/solution.py
@@ -422,23 +422,32 @@
     section_tiles(section, flow_y, flow_z, partial, range(1, 1 + rows // SUB), emit)
 
 
-def last_kernel(partial, strips, packed, result):
+def terms_kernel(strips, packed, terms):
     _, begins, last = axis_place("rad")
-    _, layers, rows, cols = partial.shape
-    lane = lax.rem(lanes_of((rows, cols)), cols // layers)
+    _, rows, cols = strips.shape
+    lane = lax.rem(lanes_of((rows, cols)), 2 * RIGHT)
     halo = []
     for f in range(FIELDS):
         ghosts = packed[f // 4]
         left = jnp.where(begins, move(ghosts, REACH - (f % 4) * PACK), strips[f])
         right = jnp.where(last, move(ghosts, 2 * REACH - (f % 4) * PACK), strips[f])
         halo.append(ends_strip(left, right, lane))
-    terms = end_terms(halo, layers)
+    for f, term in enumerate(end_terms(halo, cols // (2 * RIGHT))):
+        terms[f] = 0.5 * time_step * term
+
+
+def last_kernel(partial, terms, result, final, sems):
+    _, layers, rows, cols = partial.shape
     column = lanes_of((rows, cols))
     ends = (column < REACH) | (column >= cols - REACH)
+    copies = []
     for f in range(FIELDS):
         for z in range(layers):
-            added = jnp.where(ends, 0.5 * time_step * to_plane(terms[f], z, layers), 0.0)
-            result[f, z] = partial[f, z] + added
+            final[f, z] = partial[f, z] + jnp.where(ends, to_plane(terms[f], z, layers), 0.0)
+        copies.append(pltpu.make_async_copy(final.at[f], result.at[f], sems.at[f]))
+        copies[f].start()
+    for copy in copies:
+        copy.wait()
 
 
 VMEM = pl.BlockSpec(memory_space=pltpu.VMEM)
@@ -562,7 +571,7 @@
         section,
         scratch=[(FIELDS, layers, height, cols)] * 3,
     )
-    return call(last_kernel, "second_ends", struct(FIELDS, layers, rows, cols), partial, strips, packed)
+    return partial, call(terms_kernel, "second_terms", struct(FIELDS, rows, cols), strips, packed)
 
 
 def shards(density, momentum, magnetic, tracer, offsets):
@@ -587,7 +596,17 @@
     branches = [
         functools.partial(exchange_and_step, wrap, turned_wrap) for wrap in range(2) for turned_wrap in range(2)
     ]
-    return lax.switch(index[0], branches, shifts, state, near, far, pairs, *bulks)
+    partial, terms = lax.switch(index[0], branches, shifts, state, near, far, pairs, *bulks)
+    return call(
+        last_kernel,
+        "second_ends",
+        struct(FIELDS, layers, rows, cols),
+        partial,
+        terms,
+        scratch=[(FIELDS, layers, rows, cols)],
+        sems=FIELDS,
+        out_spec=HBM,
+    )
 
 
 def solution(mesh):

time: 20.9 us -> 21 us (level)
  starting transfers between devices: 12.6 us -> 9.85 us
  waiting for transfers between devices: 2.28 us -> 4.88 us
  Pallas kernels: 4.83 us -> 5.59 us
  local copies, waits for them, and re-layouts: 0.7 us -> 0 us
    ppermute x1, starting transfers between devices: 1.86 us -> 0.05 us  [exchange_and_step(): packed = lax.ppermute(packed, axes, turn_route)]
    ppermute x1, starting transfers between devices: 2.55 us -> 0.8 us  [exchange_and_step(): second = lax.ppermute(for_second, axes, second_route)]
    ppermute x1, waiting for transfers between devices: 0.43 us -> 1.63 us  [exchange_and_step(): packed = lax.ppermute(packed, axes, turn_route)]
    ppermute x1, waiting for transfers between devices: 1.16 us -> 2.33 us  [exchange_and_step(): second = lax.ppermute(for_second, axes, second_route)]
    ppermute x1, starting transfers between devices: 0.07 us -> 0.87 us  [exchange_and_step(): first = lax.ppermute(for_first, axes, first_route)]
    pallas_call x6 -> x7, Pallas kernels: 3.49 us -> 4.25 us  [call(): pl.pallas_call(kernel, name=name, out_shape=outs, in_specs=[SMEM] * smem...]
    unnamed x2 -> x0, local copies, waits for them, and re-layouts: 0.7 us -> none
    ppermute x2, waiting for transfers between devices: 0.01 us -> 0.24 us  [exchange_and_step(): lax.ppermute(part, axes, (first_route, second_route)[i])]
  transfers between devices with their start and end apart: 7 -> 7, of which waited for: 3 -> 4; matrix products, arithmetic and copies ran while one was open for 0% -> 0% of each run, Pallas kernels for 13% -> 13%
where the time goes in v5:
time: 21 us; the launch traced here: 20.8 us
  starting transfers between devices  9.85 us (47%)
  Pallas kernels  5.59 us (27%)
  waiting for transfers between devices  4.88 us (23%)
  loops' own time  0.29 us (1%)
    pallas_call x7, Pallas kernels, call(): pl.pallas_call(kernel, name=name, out_shape=outs, in_specs=[SMEM] * smem...  4.25 us
    ppermute x1, starting transfers between devices, exchange_and_step(): far_in = lax.ppermute(far, axes, far_route)  3.09 us
    ppermute x2, starting transfers between devices, exchange_and_step(): lax.ppermute(part, axes, (first_route, second_route)[i])  2.56 us
    ppermute x1, starting transfers between devices, exchange_and_step(): near_in = lax.ppermute(near, axes, near_route)  2.47 us
    ppermute x1, waiting for transfers between devices, exchange_and_step(): second = lax.ppermute(for_second, axes, second_route)  2.33 us
    ppermute x1, waiting for transfers between devices, exchange_and_step(): packed = lax.ppermute(packed, axes, turn_route)  1.63 us
    pallas_call x1, Pallas kernels, shards(): pl.pallas_call(edges_kernel, name='edges', out_shape=[struct(FIELDS, laye...  1.34 us
    ppermute x1, starting transfers between devices, exchange_and_step(): first = lax.ppermute(for_first, axes, first_route)  0.87 us
  transfers between devices with their start and end apart: 7, of which 4 were waited for; matrix products, arithmetic and copies ran while one was open for 0% of the time, Pallas kernels for 13%

profile of v5, /device:TPU:0, one launch (start us, length us, event | category | flops | bytes accessed | tf_op | source)
XLA Modules:
  0.0 20.8 jit_solution(5788741248354683676)
XLA Ops:
  0.0 1.3 %edges.1 = (f32[8,4,16,128]{3,2,1,0:T(8,128)S(1)}, f32[4,16,128]{2,1,0:T(8,128)S(1)}, f32[6,16,128]{2,1,0:T(8,128)S(1)}, f32[4,16,128]{2,1,0:T(8,128)S(1)}, s32[...) custom-call(f32[4,16,128]{2,1,0:T(8,128)} %density.1, ...), custom_call_target="tpu_custom_call" | custom-call | tf_op jit(solution)/shard_map/edges/pallas_call | solution.py:579
  1.4 18.4 %conditional.1 = (f32[8,4,16,128]{3,2,1,0:T(8,128)S(1)}, f32[8,16,128]{2,1,0:T(8,128)S(1)}) conditional(s32[]{:T(128)} %bitcast, (f32[4,16,128]{2,1,0:T(8,128)S(1)}, f32[6,16,128]{2,1,0:T(8,128)S(1)}, f32[4,16,128]{2,1,0:T(8,128)S(1)}, f32[192,128]{1,0:T(8,128)S(1)}, f32[192,128]{1,0:T(8,128)S(1)}, ...), branch_computations={%region_0.0_spmd, %region_1.0_spmd, %region_2.0_spmd, %region_3.0_... | conditional | bytes 3277096 | solution.py:599
  1.4 3.1 %collective-permute-start.8 = (f32[6,16,128]{2,1,0:T(8,128)S(1)}, f32[6,16,128]{2,1,0:T(8,128)S(1)}, u32[]{:S(2)}, u32[]{:S(2)}) collective-permute-start(f32[6,16,128]{2,1,0:T(8,128)S(1)} %get-tuple-element.78), channel_id=1, source_target_pairs={{0,1},{1,0},{2,3},{3,2},{4,5},{5,4},{6,7},{7,6},{8,9},{9,8},{10,11... | collective-permute-start | bytes 147464 | tf_op jit(solution)/shard_map/cond/branch_1_fun/ppermute | solution.py:516
  4.5 2.5 %collective-permute-start.7 = (f32[4,16,128]{2,1,0:T(8,128)S(1)}, f32[4,16,128]{2,1,0:T(8,128)S(1)}, u32[]{:S(2)}, u32[]{:S(2)}) collective-permute-start(f32[4,16,128]{2,1,0:T(8,128)S(1)} %get-tuple-element.77), channel_id=1, source_target_pairs={{0,3},{1,2},{2,1},{3,0},{4,7},{5,6},{6,5},{7,4},{8,11},{9,10},{10,... | collective-permute-start | bytes 98312 | tf_op jit(solution)/shard_map/cond/branch_1_fun/ppermute | solution.py:517
  6.9 0.0 collective-permute-start.11
  6.9 2.6 %collective-permute-start.12 = (f32[192,128]{1,0:T(8,128)S(1)}, f32[192,128]{1,0:T(8,128)S(1)}, u32[]{:S(2)}, u32[]{:S(2)}) collective-permute-start(f32[192,128]{1,0:T(8,128)S(1)} %get-tuple-element.84), channel_id=1, source_target_pairs={{0,28},{1,29},{2,30},{3,31},{4,8},{5,9},{6,10},{7,11},{8,4},{9,5},... | collective-permute-start | bytes 294920 | tf_op jit(solution)/shard_map/cond/branch_1_fun/ppermute | solution.py:518
  9.5 0.7 %collective-permute-done.7.near = f32[4,16,128]{2,1,0:T(8,128)S(1)} collective-permute-done((f32[4,16,128]{2,1,0:T(8,128)S(1)}, f32[4,16,128]{2,1,0:T(8,128)S(1)}, u32[]{:S(2)}, u32[]{:S(2)}) %collective-permute-start.7) | collective-permute-done | bytes 32800 | tf_op jit(solution)/shard_map/cond/branch_1_fun/ppermute | solution.py:517
  10.2 0.0 collective-permute-done.8.far
  10.2 0.1 join.5
  10.3 0.8 %collective-permute-start.10 = (f32[16,8,128]{2,1,0:T(8,128)S(1)}, f32[16,8,128]{2,1,0:T(8,128)S(1)}, u32[]{:S(2)}, u32[]{:S(2)}) collective-permute-start(f32[16,8,128]{2,1,0:T(8,128)S(1)} %get-tuple-element.81), channel_id=1, source_target_pairs={{0,28},{1,29},{2,30},{3,31},{4,8},{5,9},{6,10},{7,11},{8,4},{9,5},... | collective-permute-start | bytes 196616 | tf_op jit(solution)/shard_map/cond/branch_1_fun/ppermute | solution.py:529
  11.1 0.9 %collective-permute-start.9 = (f32[16,8,128]{2,1,0:T(8,128)S(1)}, f32[16,8,128]{2,1,0:T(8,128)S(1)}, u32[]{:S(2)}, u32[]{:S(2)}) collective-permute-start(f32[16,8,128]{2,1,0:T(8,128)S(1)} %get-tuple-element.80), channel_id=1, source_target_pairs={{0,4},{1,5},{2,6},{3,7},{4,0},{5,1},{6,2},{7,3},{8,12},{9,13},{10,... | collective-permute-start | bytes 196616 | tf_op jit(solution)/shard_map/cond/branch_1_fun/ppermute | solution.py:528
  12.0 0.0 collective-permute-done.11.first
  12.0 0.2 %collective-permute-done.12.second = f32[192,128]{1,0:T(8,128)S(1)} collective-permute-done((f32[192,128]{1,0:T(8,128)S(1)}, f32[192,128]{1,0:T(8,128)S(1)}, u32[]{:S(2)}, u32[]{:S(2)}) %collective-permute-start.12) | collective-permute-done | bytes 98336 | tf_op jit(solution)/shard_map/cond/branch_1_fun/ppermute | solution.py:518
  12.2 1.0 %first_section.5.partial._ = f32[8,4,32,128]{3,2,1,0:T(8,128)S(1)} custom-call(f32[8,4,16,128]{3,2,1,0:T(8,128)S(1)} %get-tuple-element.74.state, f32[192,128]{1,0:T(8,128)S(1)} %collective-permute-done.11.first, f32[192,128]{1,0:T(8,128)S(1)} %collective-permute-done.12.second), custom_call_target="tpu_custom_call" | custom-call | bytes 262144 | tf_op jit(solution)/shard_map/cond/branch_1_fun/first_section/pallas_call | solution.py:466
  13.2 2.3 %collective-permute-done.10.second = f32[16,8,128]{2,1,0:T(8,128)S(1)} collective-permute-done((f32[16,8,128]{2,1,0:T(8,128)S(1)}, f32[16,8,128]{2,1,0:T(8,128)S(1)}, u32[]{:S(2)}, u32[]{:S(2)}) %collective-permute-start.10) | collective-permute-done | bytes 65568 | tf_op jit(solution)/shard_map/cond/branch_1_fun/ppermute | solution.py:529
  15.6 0.0 collective-permute-done.9.first
  15.6 0.5 %far.5 = f32[2,16,128]{2,1,0:T(8,128)S(1)} custom-call(s32[8,128]{1,0:T(8,128)S(1)} %get-tuple-element.75.shifts.offsets, f32[4,16,128]{2,1,0:T(8,128)S(1)} %get-tuple-element.79.own, f32[16,8,128]{2,1,0:T(8,128)S(1)} %collective-permute-done.9.first, f32[16,8,128]{2,1,0:T(8,128)S(1)} %collective-permute-done.10.second, ...), custom_call_target="tpu_custom_call" | custom-call | bytes 262144 | tf_op jit(solution)/shard_map/cond/branch_1_fun/far/pallas_call | solution.py:466
  16.1 0.1 collective-permute-start.13
  16.2 1.0 %first_ends.5 = (f32[8,4,32,128]{3,2,1,0:T(8,128)S(1)}, f32[8,16,128]{2,1,0:T(8,128)S(1)}) custom-call(s32[8,128]{1,0:T(8,128)S(1)} %get-tuple-element.75.shifts.offsets, f32[8,4,16,128]{3,2,1,0:T(8,128)S(1)} %get-tuple-element.74.state, f32[4,16,128]{2,1,0:T(8,128)S(1)} %get-tuple-element.79.own, f32[16,8,128]{2,1,0:T(8,128)S(1)} %collective-permute-done.9.first, ...), custom_call_target="tpu_custom_call" | custom-call | bytes 262144 | tf_op jit(solution)/shard_map/cond/branch_1_fun/first_ends/pallas_call | solution.py:466
  17.1 0.6 %second_section.5 = f32[8,4,16,128]{3,2,1,0:T(8,128)S(1)} custom-call(f32[8,4,16,128]{3,2,1,0:T(8,128)S(1)} %get-tuple-element.74.state, f32[8,4,32,128]{3,2,1,0:T(8,128)S(1)} %get-tuple-element.85.section), custom_call_target="tpu_custom_call" | custom-call | bytes 262144 | tf_op jit(solution)/shard_map/cond/branch_1_fun/second_section/pallas_call | solution.py:466
  17.7 1.6 %collective-permute-done.13.packed = f32[2,16,128]{2,1,0:T(8,128)S(1)} collective-permute-done((f32[2,16,128]{2,1,0:T(8,128)S(1)}, f32[2,16,128]{2,1,0:T(8,128)S(1)}, u32[]{:S(2)}, u32[]{:S(2)}) %collective-permute-start.13) | collective-permute-done | bytes 16416 | tf_op jit(solution)/shard_map/cond/branch_1_fun/ppermute | solution.py:552
  19.3 0.3 %second_terms.5 = f32[8,16,128]{2,1,0:T(8,128)S(1)} custom-call(f32[8,16,128]{2,1,0:T(8,128)S(1)} %get-tuple-element.86.strips, f32[2,16,128]{2,1,0:T(8,128)S(1)} %collective-permute-done.13.packed), custom_call_target="tpu_custom_call" | custom-call | bytes 262144 | tf_op jit(solution)/shard_map/cond/branch_1_fun/second_terms/pallas_call | solution.py:466
  19.8 0.8 %second_ends.1 = f32[8,4,16,128]{3,2,1,0:T(8,128)} custom-call(f32[8,4,16,128]{3,2,1,0:T(8,128)S(1)} %get-tuple-element.131.partial, f32[8,16,128]{2,1,0:T(8,128)S(1)} %get-tuple-element.132.terms), custom_call_target="tpu_custom_call" | custom-call | bytes 262144 | tf_op jit(solution)/shard_map/second_ends/pallas_call | solution.py:466
Async XLA Ops:
  1.4 8.8 %collective-permute-start.8 = (f32[6,16,128]{2,1,0:T(8,128)S(1)}, f32[6,16,128]{2,1,0:T(8,128)S(1)}, u32[]{:S(2)}, u32[]{:S(2)}) collective-permute-start(f32[6,16,128]{2,1,0:T(8,128)S(1)} %get-tuple-element.78), channel_id=1, source_target_pairs={{0,1},{1,0},{2,3},{3,2},{4,5},{5,4},{6,7},{7,6},{8,9},{9,8},{10,11... | collective-permute-start | bytes 147464 | tf_op jit(solution)/shard_map/cond/branch_1_fun/ppermute | solution.py:516
  4.5 5.7 %collective-permute-start.7 = (f32[4,16,128]{2,1,0:T(8,128)S(1)}, f32[4,16,128]{2,1,0:T(8,128)S(1)}, u32[]{:S(2)}, u32[]{:S(2)}) collective-permute-start(f32[4,16,128]{2,1,0:T(8,128)S(1)} %get-tuple-element.77), channel_id=1, source_target_pairs={{0,3},{1,2},{2,1},{3,0},{4,7},{5,6},{6,5},{7,4},{8,11},{9,10},{10,... | collective-permute-start | bytes 98312 | tf_op jit(solution)/shard_map/cond/branch_1_fun/ppermute | solution.py:517
  6.9 5.0 %collective-permute-start.11 = (f32[192,128]{1,0:T(8,128)S(1)}, f32[192,128]{1,0:T(8,128)S(1)}, u32[]{:S(2)}, u32[]{:S(2)}) collective-permute-start(f32[192,128]{1,0:T(8,128)S(1)} %get-tuple-element.83), channel_id=1, source_target_pairs={{0,4},{1,5},{2,6},{3,7},{4,0},{5,1},{6,2},{7,3},{8,12},{9,13},{10,... | collective-permute-start | bytes 294920 | tf_op jit(solution)/shard_map/cond/branch_1_fun/ppermute | solution.py:518
  6.9 5.3 %collective-permute-start.12 = (f32[192,128]{1,0:T(8,128)S(1)}, f32[192,128]{1,0:T(8,128)S(1)}, u32[]{:S(2)}, u32[]{:S(2)}) collective-permute-start(f32[192,128]{1,0:T(8,128)S(1)} %get-tuple-element.84), channel_id=1, source_target_pairs={{0,28},{1,29},{2,30},{3,31},{4,8},{5,9},{6,10},{7,11},{8,4},{9,5},... | collective-permute-start | bytes 294920 | tf_op jit(solution)/shard_map/cond/branch_1_fun/ppermute | solution.py:518
  10.3 5.3 %collective-permute-start.10 = (f32[16,8,128]{2,1,0:T(8,128)S(1)}, f32[16,8,128]{2,1,0:T(8,128)S(1)}, u32[]{:S(2)}, u32[]{:S(2)}) collective-permute-start(f32[16,8,128]{2,1,0:T(8,128)S(1)} %get-tuple-element.81), channel_id=1, source_target_pairs={{0,28},{1,29},{2,30},{3,31},{4,8},{5,9},{6,10},{7,11},{8,4},{9,5},... | collective-permute-start | bytes 196616 | tf_op jit(solution)/shard_map/cond/branch_1_fun/ppermute | solution.py:529
  11.1 4.5 %collective-permute-start.9 = (f32[16,8,128]{2,1,0:T(8,128)S(1)}, f32[16,8,128]{2,1,0:T(8,128)S(1)}, u32[]{:S(2)}, u32[]{:S(2)}) collective-permute-start(f32[16,8,128]{2,1,0:T(8,128)S(1)} %get-tuple-element.80), channel_id=1, source_target_pairs={{0,4},{1,5},{2,6},{3,7},{4,0},{5,1},{6,2},{7,3},{8,12},{9,13},{10,... | collective-permute-start | bytes 196616 | tf_op jit(solution)/shard_map/cond/branch_1_fun/ppermute | solution.py:528
  16.1 3.2 %collective-permute-start.13 = (f32[2,16,128]{2,1,0:T(8,128)S(1)}, f32[2,16,128]{2,1,0:T(8,128)S(1)}, u32[]{:S(2)}, u32[]{:S(2)}) collective-permute-start(f32[2,16,128]{2,1,0:T(8,128)S(1)} %far.5), channel_id=1, source_target_pairs={{0,12},{1,17},{2,18},{3,23},{4,16},{5,21},{6,22},{7,27},{8,20},{9,... | collective-permute-start | bytes 49160 | tf_op jit(solution)/shard_map/cond/branch_1_fun/ppermute | solution.py:552
